TPU v7x, 32 devices: a whole 2x2x4 slice. The times are simulated.
32 devices in a mesh: qrow: 8 (over z, core), kcol: 4 (over y, x).
Axes of the slice: x: 2, y: 2, z: 4, core: 2. Of those that a mesh axis runs over, the one named last changes fastest.
Arguments:
- queries: bfloat16 [4096, 1024], P(('kcol', 'qrow')), may hold values from -105 to 105
- keys: bfloat16 [4096, 256], P(('qrow', 'kcol')), may hold values from -3.5 to 3.5
- values: bfloat16 [4096, 256], P(('qrow', 'kcol')), may hold values from -6 to 6
- outputs: bfloat16 [4096, 1024], P(('kcol', 'qrow')), may hold values from -6 to 6
- out_grad: bfloat16 [4096, 1024], P(('kcol', 'qrow')), may hold values from -6 to 6
- positions: int32 [4096], replicated, may hold values from 0 to 4095, as said below
Outputs:
- query_grad: bfloat16 [4096, 1024], P(('kcol', 'qrow'))
- key_grad: bfloat16 [4096, 256], P(('qrow', 'kcol'))
- value_grad: bfloat16 [4096, 256], P(('qrow', 'kcol'))
Inputs may be any that keep to these rules, and one draw needn't show every extreme that they name: positions is a permutation of the 4096 positions; each aligned run of 64 stored rows holds consecutive positions in increasing order, the first a multiple of 64.
All inputs are finite; a program needn't handle non-finite values.
Results may differ from a plain program's by a relative error of at most 0.0048.
Values may be sent and summed in bfloat16 or wider, within the bound.
A program may use at most 128 MiB of HBM per device.

v0:
```python
import math

import jax
import jax.numpy as jnp
from jax import lax
from jax.sharding import PartitionSpec as P

HEADS = 16
KV_HEADS = 4
HEAD = 64


def merged_2(array, axis, combine):
    everything = jax.tree.map(lambda part: lax.all_gather(part, axis), array)
    leading = jax.tree.map(lambda part: part[0], everything)

    def lap(k, so_far):
        return combine(so_far, jax.tree.map(lambda part: part[k], everything))

    return lax.fori_loop(1, lax.axis_size(axis), lap, leading)


def combine_stats(first_pair, second_pair):
    first_top, first_total = first_pair
    second_top, second_total = second_pair
    joined = jnp.maximum(first_top, second_top)
    merged = first_total * jnp.exp(first_top - joined) + second_total * jnp.exp(second_top - joined)
    return (joined, merged)


def per_device(queries, keys, values, outputs, out_grad, positions):
    factor = 1.0 / math.sqrt(HEAD)
    members = HEADS // KV_HEADS
    group_width = members * HEAD
    local_rows = queries.shape[0]
    row_size = lax.axis_size("qrow")
    own_terms = jnp.sum(
        out_grad.astype(jnp.float32).reshape(-1, HEADS, HEAD)
        * outputs.astype(jnp.float32).reshape(-1, HEADS, HEAD),
        axis=2,
    )
    key_block, value_block = (
        lax.all_gather(keys, "kcol", axis=0, tiled=True),
        lax.all_gather(values, "kcol", axis=0, tiled=True),
    )
    gathered_delta = lax.all_gather(own_terms, "qrow", axis=0, tiled=True)
    query_span = local_rows * row_size
    key_span = key_block.shape[0]
    query_pos = lax.dynamic_slice_in_dim(positions, lax.axis_index("kcol") * query_span, query_span)
    key_pos = lax.dynamic_slice_in_dim(positions, lax.axis_index("qrow") * key_span, key_span)
    query_count = query_pos.shape[0]
    key_count = key_block.shape[0]
    visible = key_pos[None, :] <= query_pos[:, None]

    def group_step(unused, kv_index):
        column = kv_index * group_width
        query_cols = lax.dynamic_slice_in_dim(queries, column, group_width, 1)
        grad_cols = lax.dynamic_slice_in_dim(out_grad, column, group_width, 1)
        query_full, grad_full = (
            lax.all_gather(query_cols, "qrow", axis=0, tiled=True),
            lax.all_gather(grad_cols, "qrow", axis=0, tiled=True),
        )
        delta_full = lax.dynamic_slice_in_dim(gathered_delta, kv_index * members, members, 1)
        query_heads = query_full.reshape(query_count, members, HEAD)
        grad_heads = grad_full.reshape(query_count, members, HEAD)
        key_head = lax.dynamic_slice_in_dim(key_block, kv_index * HEAD, HEAD, 1)
        value_head = lax.dynamic_slice_in_dim(value_block, kv_index * HEAD, HEAD, 1)

        def pair_scores(first):
            raw_scores = (
                jnp.einsum(
                    "qhd,kd->hqk",
                    query_heads[:, first : first + 2],
                    key_head,
                    preferred_element_type=jnp.float32,
                )
                * factor
            )
            return jnp.where(visible[None], raw_scores, jnp.float32(-1e30))

        maxima = []
        totals = []
        for first in range(0, members, 2):
            scores = pair_scores(first)
            pair_top = jnp.max(scores, axis=2)
            maxima.append(pair_top)
            totals.append(
                jnp.sum(
                    jnp.where(
                        visible[None], jnp.exp(scores - pair_top[:, :, None]), jnp.float32(0.0)
                    ),
                    axis=2,
                )
            )
        local_top = jnp.concatenate(maxima, axis=0)
        local_total = jnp.concatenate(totals, axis=0)
        top_score, row_sum = merged_2((local_top, local_total), "qrow", combine_stats)
        log_total = top_score + jnp.log(row_sum)
        key_total = jnp.zeros((key_count, HEAD), jnp.float32)
        value_total = jnp.zeros((key_count, HEAD), jnp.float32)
        pieces = []
        for first in range(0, members, 2):
            scores = pair_scores(first)
            weights = jnp.exp(scores - log_total[first : first + 2, :, None])
            pair_grad = grad_heads[:, first : first + 2]
            value_total = value_total + jnp.einsum(
                "hqk,qhd->kd",
                weights.astype(jnp.bfloat16),
                pair_grad,
                preferred_element_type=jnp.float32,
            )
            dweight = jnp.einsum(
                "qhd,kd->hqk", pair_grad, value_head, preferred_element_type=jnp.float32
            )
            pair_delta = jnp.transpose(delta_full[:, first : first + 2])[:, :, None]
            dscore = (weights * (dweight - pair_delta) * factor).astype(jnp.bfloat16)
            pieces.append(
                jnp.einsum("hqk,kd->qhd", dscore, key_head, preferred_element_type=jnp.float32)
            )
            key_total = key_total + jnp.einsum(
                "hqk,qhd->kd",
                dscore,
                query_heads[:, first : first + 2],
                preferred_element_type=jnp.float32,
            )
        query_total = jnp.concatenate(pieces, axis=1).reshape(query_count, group_width)
        query_share = lax.psum_scatter(query_total, "qrow", scatter_dimension=0, tiled=True)
        key_share, value_share = (
            lax.psum_scatter(key_total, "kcol", scatter_dimension=0, tiled=True),
            lax.psum_scatter(value_total, "kcol", scatter_dimension=0, tiled=True),
        )
        return (unused, (query_share, key_share, value_share))

    ignored, shares = lax.scan(
        group_step, jnp.zeros((), jnp.float32), jnp.arange(KV_HEADS, dtype=jnp.int32)
    )
    query_parts, key_parts, value_parts = shares
    query_grad = (
        jnp.transpose(query_parts, (1, 0, 2))
        .reshape(query_parts.shape[1], HEADS * HEAD)
        .astype(jnp.bfloat16)
    )
    key_grad = (
        jnp.transpose(key_parts, (1, 0, 2))
        .reshape(key_parts.shape[1], KV_HEADS * HEAD)
        .astype(jnp.bfloat16)
    )
    value_grad = (
        jnp.transpose(value_parts, (1, 0, 2))
        .reshape(value_parts.shape[1], KV_HEADS * HEAD)
        .astype(jnp.bfloat16)
    )
    return (query_grad, key_grad, value_grad)


def solution(mesh):
    in_specs = (
        P(("kcol", "qrow"), None),
        P(("qrow", "kcol"), None),
        P(("qrow", "kcol"), None),
        P(("kcol", "qrow"), None),
        P(("kcol", "qrow"), None),
        P(),
    )
    out_specs = (P(("kcol", "qrow"), None), P(("qrow", "kcol"), None), P(("qrow", "kcol"), None))
    return jax.shard_map(
        per_device, mesh=mesh, in_specs=in_specs, out_specs=out_specs, check_vma=False
    )
```

profile of v0, /device:TPU:0, one launch (start us, length us, event | category | flops | bytes accessed | tf_op | source)
XLA Modules:
  0.0 691.7 jit_solution(9834017042577956576)
XLA Ops:
  8.6 1.8 copy.48
  12.6 15.6 %all_gather.47 = f32[1024,16]{0,1:T(8,128)S(1)} all-gather(f32[128,16]{0,1:T(8,128)S(1)} %bitcast_reduce_fusion), channel_id=1, replica_groups=mesh['qrow'=8,'kcol'=4] {'qrow'}, dimensions={0}, use_global_device_ids=true | all-gather | bytes 73728 | tf_op jit(solution)/shard_map/all_gather | solution.py:46
  29.2 9.0 %all_gather.45 = bf16[512,256]{0,1:T(8,128)(2,1)S(1)} all-gather(bf16[128,256]{0,1:T(8,128)(2,1)S(1)} %copy.43), channel_id=1, replica_groups=mesh['qrow'=8,'kcol'=4] {'kcol'}, dimensions={0}, use_global_device_ids=true | all-gather | bytes 327680 | tf_op jit(solution)/shard_map/all_gather | solution.py:43
  39.1 9.9 %all_gather.46 = bf16[512,256]{0,1:T(8,128)(2,1)} all-gather(bf16[128,256]{0,1:T(8,128)(2,1)S(1)} %copy.44), channel_id=1, replica_groups=mesh['qrow'=8,'kcol'=4] {'kcol'}, dimensions={0}, use_global_device_ids=true | all-gather | bytes 327680 | tf_op jit(solution)/shard_map/all_gather | solution.py:44
  49.0 630.9 %while.45 = (s32[]{:T(128)}, bf16[4,128,256]{1,2,0:T(8,128)(2,1)}, bf16[4,128,64]{1,2,0:T(8,128)(2,1)}, bf16[4,128,64]{1,2,0:T(8,128)(2,1)}, s32[4]{0:T(128)S(1)...) while((s32[]{:T(128)}, bf16[4,128,256]{1,2,0:T(8,128)(2,1)}, ...), condition=%wide.region_11.12_spmd.clone, body=%wide.region_1.11_spmd.clone.sunk | while | flops 1382903808 | bytes 143678400 | solution.py:134
  51.3 14.3 %all_gather.52 = bf16[1024,256]{0,1:T(8,128)(2,1)S(1)} all-gather(bf16[128,256]{0,1:T(8,128)(2,1)S(1)} %copy.61), channel_id=1, replica_groups=mesh['qrow'=8,'kcol'=4] {'qrow'}, dimensions={0}, use_global_device_ids=true | all-gather | bytes 589824 | tf_op jit(solution)/shard_map/while/body/eval_jaxpr/all_gather | solution.py:60
  67.6 2.0 select_reduce_fusion.4
  69.6 1.9 copy-done.1
  72.7 14.0 %all-gather.9 = f32[8,4,1024]{2,1,0:T(4,128)S(1)} all-gather(f32[1,4,1024]{2,1,0:T(4,128)S(1)} %maximum_bitcast_fusion.5), channel_id=3, replica_groups=mesh['qrow'=8,'kcol'=4] {'qrow'}, dimensions={0}, use_global_device_ids=true | all-gather | bytes 147456 | tf_op jit(solution)/shard_map/while/body/eval_jaxpr/all_gather | solution.py:14
  86.6 13.9 %all-gather.8 = f32[8,4,1024]{2,1,0:T(4,128)S(1)} all-gather(f32[1,4,1024]{2,1,0:T(4,128)S(1)} %maximum_bitcast_fusion.4), channel_id=2, replica_groups=mesh['qrow'=8,'kcol'=4] {'qrow'}, dimensions={0}, use_global_device_ids=true | all-gather | bytes 147456 | tf_op jit(solution)/shard_map/while/body/eval_jaxpr/all_gather | solution.py:14
  102.0 14.1 %all_gather.53 = bf16[1024,256]{0,1:T(8,128)(2,1)S(1)} all-gather(bf16[128,256]{0,1:T(8,128)(2,1)S(1)} %constant_dynamic-slice_fusion.5), channel_id=1, replica_groups=mesh['qrow'=8,'kcol'=4] {'qrow'}, dimensions={0}, use_global_device_ids=true | all-gather | bytes 589824 | tf_op jit(solution)/shard_map/while/body/eval_jaxpr/all_gather | solution.py:61
  116.1 3.6 fusion.112
  119.7 1.9 fusion.113
  122.5 4.1 fusion.110
  126.6 2.6 fusion.109
  133.3 2.1 convolution_bitcast_fusion.7
  136.5 6.8 reduce-scatter.8.cloned.1.call-done
  144.6 25.3 %reduce-scatter.6.cloned.1.call-done = f32[128,64]{0,1:T(8,128)} async-done(((f32[512,64]{0,1:T(8,128)}), f32[128,64]{0,1:T(8,128)}) %reduce-scatter.6.cloned.1.call-update) | async-done | bytes 32784 | tf_op jit(solution)/shard_map/while/body/eval_jaxpr/reduce_scatter | solution.py:129
  171.3 33.3 %reduce-scatter.4.cloned.1.call-done = f32[128,256]{0,1:T(8,128)} async-done(((f32[1024,256]{0,1:T(8,128)}), f32[128,256]{0,1:T(8,128)}) %reduce-scatter.4.cloned.1.call-update) | async-done | bytes 131088 | tf_op jit(solution)/shard_map/while/body/eval_jaxpr/reduce_scatter | solution.py:127
  208.3 14.0 %all_gather.52 = bf16[1024,256]{0,1:T(8,128)(2,1)S(1)} all-gather(bf16[128,256]{0,1:T(8,128)(2,1)S(1)} %copy.61), channel_id=1, replica_groups=mesh['qrow'=8,'kcol'=4] {'qrow'}, dimensions={0}, use_global_device_ids=true | all-gather | bytes 589824 | tf_op jit(solution)/shard_map/while/body/eval_jaxpr/all_gather | solution.py:60
  224.3 2.0 select_reduce_fusion.4
  226.4 1.9 copy-done.1
  229.4 14.0 %all-gather.9 = f32[8,4,1024]{2,1,0:T(4,128)S(1)} all-gather(f32[1,4,1024]{2,1,0:T(4,128)S(1)} %maximum_bitcast_fusion.5), channel_id=3, replica_groups=mesh['qrow'=8,'kcol'=4] {'qrow'}, dimensions={0}, use_global_device_ids=true | all-gather | bytes 147456 | tf_op jit(solution)/shard_map/while/body/eval_jaxpr/all_gather | solution.py:14
  243.4 14.0 %all-gather.8 = f32[8,4,1024]{2,1,0:T(4,128)S(1)} all-gather(f32[1,4,1024]{2,1,0:T(4,128)S(1)} %maximum_bitcast_fusion.4), channel_id=2, replica_groups=mesh['qrow'=8,'kcol'=4] {'qrow'}, dimensions={0}, use_global_device_ids=true | all-gather | bytes 147456 | tf_op jit(solution)/shard_map/while/body/eval_jaxpr/all_gather | solution.py:14
  258.8 14.3 %all_gather.53 = bf16[1024,256]{0,1:T(8,128)(2,1)S(1)} all-gather(bf16[128,256]{0,1:T(8,128)(2,1)S(1)} %constant_dynamic-slice_fusion.5), channel_id=1, replica_groups=mesh['qrow'=8,'kcol'=4] {'qrow'}, dimensions={0}, use_global_device_ids=true | all-gather | bytes 589824 | tf_op jit(solution)/shard_map/while/body/eval_jaxpr/all_gather | solution.py:61
  273.1 3.6 fusion.112
  276.8 1.9 fusion.113
  279.5 4.1 fusion.110
  283.7 2.6 fusion.109
  290.3 2.1 convolution_bitcast_fusion.7
  293.6 7.8 %reduce-scatter.8.cloned.1.call-done = f32[128,64]{0,1:T(8,128)} async-done(((f32[512,64]{0,1:T(8,128)}), f32[128,64]{0,1:T(8,128)}) %reduce-scatter.8.cloned.1.call-update) | async-done | bytes 32784 | tf_op jit(solution)/shard_map/while/body/eval_jaxpr/reduce_scatter | solution.py:130
  302.8 25.1 %reduce-scatter.6.cloned.1.call-done = f32[128,64]{0,1:T(8,128)} async-done(((f32[512,64]{0,1:T(8,128)}), f32[128,64]{0,1:T(8,128)}) %reduce-scatter.6.cloned.1.call-update) | async-done | bytes 32784 | tf_op jit(solution)/shard_map/while/body/eval_jaxpr/reduce_scatter | solution.py:129
  329.2 33.2 %reduce-scatter.4.cloned.1.call-done = f32[128,256]{0,1:T(8,128)} async-done(((f32[1024,256]{0,1:T(8,128)}), f32[128,256]{0,1:T(8,128)}) %reduce-scatter.4.cloned.1.call-update) | async-done | bytes 131088 | tf_op jit(solution)/shard_map/while/body/eval_jaxpr/reduce_scatter | solution.py:127
  366.2 14.0 %all_gather.52 = bf16[1024,256]{0,1:T(8,128)(2,1)S(1)} all-gather(bf16[128,256]{0,1:T(8,128)(2,1)S(1)} %copy.61), channel_id=1, replica_groups=mesh['qrow'=8,'kcol'=4] {'qrow'}, dimensions={0}, use_global_device_ids=true | all-gather | bytes 589824 | tf_op jit(solution)/shard_map/while/body/eval_jaxpr/all_gather | solution.py:60
  382.3 2.0 select_reduce_fusion.4
  384.3 1.9 copy-done.1
  387.3 14.0 %all-gather.9 = f32[8,4,1024]{2,1,0:T(4,128)S(1)} all-gather(f32[1,4,1024]{2,1,0:T(4,128)S(1)} %maximum_bitcast_fusion.5), channel_id=3, replica_groups=mesh['qrow'=8,'kcol'=4] {'qrow'}, dimensions={0}, use_global_device_ids=true | all-gather | bytes 147456 | tf_op jit(solution)/shard_map/while/body/eval_jaxpr/all_gather | solution.py:14
  401.3 14.0 %all-gather.8 = f32[8,4,1024]{2,1,0:T(4,128)S(1)} all-gather(f32[1,4,1024]{2,1,0:T(4,128)S(1)} %maximum_bitcast_fusion.4), channel_id=2, replica_groups=mesh['qrow'=8,'kcol'=4] {'qrow'}, dimensions={0}, use_global_device_ids=true | all-gather | bytes 147456 | tf_op jit(solution)/shard_map/while/body/eval_jaxpr/all_gather | solution.py:14
  416.7 14.3 %all_gather.53 = bf16[1024,256]{0,1:T(8,128)(2,1)S(1)} all-gather(bf16[128,256]{0,1:T(8,128)(2,1)S(1)} %constant_dynamic-slice_fusion.5), channel_id=1, replica_groups=mesh['qrow'=8,'kcol'=4] {'qrow'}, dimensions={0}, use_global_device_ids=true | all-gather | bytes 589824 | tf_op jit(solution)/shard_map/while/body/eval_jaxpr/all_gather | solution.py:61
  431.0 3.6 fusion.112
  434.7 1.9 fusion.113
  437.4 4.1 fusion.110
  441.6 2.6 fusion.109
  448.2 2.1 convolution_bitcast_fusion.7
  451.5 7.7 %reduce-scatter.8.cloned.1.call-done = f32[128,64]{0,1:T(8,128)} async-done(((f32[512,64]{0,1:T(8,128)}), f32[128,64]{0,1:T(8,128)}) %reduce-scatter.8.cloned.1.call-update) | async-done | bytes 32784 | tf_op jit(solution)/shard_map/while/body/eval_jaxpr/reduce_scatter | solution.py:130
  460.5 25.2 %reduce-scatter.6.cloned.1.call-done = f32[128,64]{0,1:T(8,128)} async-done(((f32[512,64]{0,1:T(8,128)}), f32[128,64]{0,1:T(8,128)}) %reduce-scatter.6.cloned.1.call-update) | async-done | bytes 32784 | tf_op jit(solution)/shard_map/while/body/eval_jaxpr/reduce_scatter | solution.py:129
  487.1 33.4 %reduce-scatter.4.cloned.1.call-done = f32[128,256]{0,1:T(8,128)} async-done(((f32[1024,256]{0,1:T(8,128)}), f32[128,256]{0,1:T(8,128)}) %reduce-scatter.4.cloned.1.call-update) | async-done | bytes 131088 | tf_op jit(solution)/shard_map/while/body/eval_jaxpr/reduce_scatter | solution.py:127
  524.2 14.0 %all_gather.52 = bf16[1024,256]{0,1:T(8,128)(2,1)S(1)} all-gather(bf16[128,256]{0,1:T(8,128)(2,1)S(1)} %copy.61), channel_id=1, replica_groups=mesh['qrow'=8,'kcol'=4] {'qrow'}, dimensions={0}, use_global_device_ids=true | all-gather | bytes 589824 | tf_op jit(solution)/shard_map/while/body/eval_jaxpr/all_gather | solution.py:60
  540.3 2.0 select_reduce_fusion.4
  542.3 1.9 copy-done.1
  545.4 14.0 %all-gather.9 = f32[8,4,1024]{2,1,0:T(4,128)S(1)} all-gather(f32[1,4,1024]{2,1,0:T(4,128)S(1)} %maximum_bitcast_fusion.5), channel_id=3, replica_groups=mesh['qrow'=8,'kcol'=4] {'qrow'}, dimensions={0}, use_global_device_ids=true | all-gather | bytes 147456 | tf_op jit(solution)/shard_map/while/body/eval_jaxpr/all_gather | solution.py:14
  559.4 14.0 %all-gather.8 = f32[8,4,1024]{2,1,0:T(4,128)S(1)} all-gather(f32[1,4,1024]{2,1,0:T(4,128)S(1)} %maximum_bitcast_fusion.4), channel_id=2, replica_groups=mesh['qrow'=8,'kcol'=4] {'qrow'}, dimensions={0}, use_global_device_ids=true | all-gather | bytes 147456 | tf_op jit(solution)/shard_map/while/body/eval_jaxpr/all_gather | solution.py:14
  574.8 14.3 %all_gather.53 = bf16[1024,256]{0,1:T(8,128)(2,1)S(1)} all-gather(bf16[128,256]{0,1:T(8,128)(2,1)S(1)} %constant_dynamic-slice_fusion.5), channel_id=1, replica_groups=mesh['qrow'=8,'kcol'=4] {'qrow'}, dimensions={0}, use_global_device_ids=true | all-gather | bytes 589824 | tf_op jit(solution)/shard_map/while/body/eval_jaxpr/all_gather | solution.py:61
  589.1 3.6 fusion.112
  592.7 1.9 fusion.113
  595.5 4.1 fusion.110
  599.6 2.6 fusion.109
  606.3 2.1 convolution_bitcast_fusion.7
  609.5 7.7 %reduce-scatter.8.cloned.1.call-done = f32[128,64]{0,1:T(8,128)} async-done(((f32[512,64]{0,1:T(8,128)}), f32[128,64]{0,1:T(8,128)}) %reduce-scatter.8.cloned.1.call-update) | async-done | bytes 32784 | tf_op jit(solution)/shard_map/while/body/eval_jaxpr/reduce_scatter | solution.py:130
  618.5 25.2 %reduce-scatter.6.cloned.1.call-done = f32[128,64]{0,1:T(8,128)} async-done(((f32[512,64]{0,1:T(8,128)}), f32[128,64]{0,1:T(8,128)}) %reduce-scatter.6.cloned.1.call-update) | async-done | bytes 32784 | tf_op jit(solution)/shard_map/while/body/eval_jaxpr/reduce_scatter | solution.py:129
  645.1 33.2 %reduce-scatter.4.cloned.1.call-done = f32[128,256]{0,1:T(8,128)} async-done(((f32[1024,256]{0,1:T(8,128)}), f32[128,256]{0,1:T(8,128)}) %reduce-scatter.4.cloned.1.call-update) | async-done | bytes 131088 | tf_op jit(solution)/shard_map/while/body/eval_jaxpr/reduce_scatter | solution.py:127
  679.9 1.8 copy.58
  681.7 1.6 copy.50
  683.2 1.6 copy.51
  (202 shorter events, 66.5 us)
Async XLA Ops:
  49.0 94.3 %reduce-scatter.8.cloned.1.call-start = ((), (), s32[]{:S(2)}) async-start(), calls=%async_computation.5 | async-start | bytes 163840 | tf_op jit(solution)/shard_map/while/body/eval_jaxpr/reduce_scatter | solution.py:130
  67.6 2.0 copy-start.6
  69.6 1.9 copy-start.1
  101.0 18.8 %copy-start.2 = (f32[512,1024,2]{1,0,2:T(8,128)S(1)}, f32[512,1024,2]{1,0,2:T(8,128)}, u32[]{:S(2)}) copy-start(f32[512,1024,2]{1,0,2:T(8,128)} %copy-done.1) | copy-start | bytes 12582916 | tf_op jit(solution)/shard_map/while
  116.1 3.6 copy-start.4
  121.7 48.2 %reduce-scatter.6.cloned.1.call-start = ((), (), s32[]{:S(2)}) async-start(), calls=%async_computation.4 | async-start | bytes 163840 | tf_op jit(solution)/shard_map/while/body/eval_jaxpr/reduce_scatter | solution.py:129
  122.4 4.2 copy-start.3
  122.4 4.2 copy-start.5
  129.2 1.4 copy-start
  132.7 71.8 %reduce-scatter.4.cloned.1.call-start = ((), (), s32[]{:S(2)}) async-start(), calls=%async_computation.3 | async-start | bytes 1179648 | tf_op jit(solution)/shard_map/while/body/eval_jaxpr/reduce_scatter | solution.py:127
  206.1 95.3 %reduce-scatter.8.cloned.1.call-start = ((), (), s32[]{:S(2)}) async-start(), calls=%async_computation.5 | async-start | bytes 163840 | tf_op jit(solution)/shard_map/while/body/eval_jaxpr/reduce_scatter | solution.py:130
  224.3 2.0 copy-start.6
  226.3 1.9 copy-start.1
  257.7 19.0 %copy-start.2 = (f32[512,1024,2]{1,0,2:T(8,128)S(1)}, f32[512,1024,2]{1,0,2:T(8,128)}, u32[]{:S(2)}) copy-start(f32[512,1024,2]{1,0,2:T(8,128)} %copy-done.1) | copy-start | bytes 12582916 | tf_op jit(solution)/shard_map/while
  273.1 3.6 copy-start.4
  278.8 49.1 %reduce-scatter.6.cloned.1.call-start = ((), (), s32[]{:S(2)}) async-start(), calls=%async_computation.4 | async-start | bytes 163840 | tf_op jit(solution)/shard_map/while/body/eval_jaxpr/reduce_scatter | solution.py:129
  279.5 4.2 copy-start.3
  279.5 4.2 copy-start.5
  286.2 1.4 copy-start
  289.8 72.7 %reduce-scatter.4.cloned.1.call-start = ((), (), s32[]{:S(2)}) async-start(), calls=%async_computation.3 | async-start | bytes 1179648 | tf_op jit(solution)/shard_map/while/body/eval_jaxpr/reduce_scatter | solution.py:127
  364.0 95.2 %reduce-scatter.8.cloned.1.call-start = ((), (), s32[]{:S(2)}) async-start(), calls=%async_computation.5 | async-start | bytes 163840 | tf_op jit(solution)/shard_map/while/body/eval_jaxpr/reduce_scatter | solution.py:130
  382.2 2.0 copy-start.6
  384.3 1.9 copy-start.1
  415.7 19.0 %copy-start.2 = (f32[512,1024,2]{1,0,2:T(8,128)S(1)}, f32[512,1024,2]{1,0,2:T(8,128)}, u32[]{:S(2)}) copy-start(f32[512,1024,2]{1,0,2:T(8,128)} %copy-done.1) | copy-start | bytes 12582916 | tf_op jit(solution)/shard_map/while
  431.0 3.6 copy-start.4
  436.7 49.1 %reduce-scatter.6.cloned.1.call-start = ((), (), s32[]{:S(2)}) async-start(), calls=%async_computation.4 | async-start | bytes 163840 | tf_op jit(solution)/shard_map/while/body/eval_jaxpr/reduce_scatter | solution.py:129
  437.4 4.2 copy-start.3
  437.4 4.2 copy-start.5
  444.2 1.4 copy-start
  447.7 72.8 %reduce-scatter.4.cloned.1.call-start = ((), (), s32[]{:S(2)}) async-start(), calls=%async_computation.3 | async-start | bytes 1179648 | tf_op jit(solution)/shard_map/while/body/eval_jaxpr/reduce_scatter | solution.py:127
  522.0 95.1 %reduce-scatter.8.cloned.1.call-start = ((), (), s32[]{:S(2)}) async-start(), calls=%async_computation.5 | async-start | bytes 163840 | tf_op jit(solution)/shard_map/while/body/eval_jaxpr/reduce_scatter | solution.py:130
  540.3 2.0 copy-start.6
  542.3 1.9 copy-start.1
  573.7 19.0 %copy-start.2 = (f32[512,1024,2]{1,0,2:T(8,128)S(1)}, f32[512,1024,2]{1,0,2:T(8,128)}, u32[]{:S(2)}) copy-start(f32[512,1024,2]{1,0,2:T(8,128)} %copy-done.1) | copy-start | bytes 12582916 | tf_op jit(solution)/shard_map/while
  589.1 3.6 copy-start.4
  594.7 49.1 %reduce-scatter.6.cloned.1.call-start = ((), (), s32[]{:S(2)}) async-start(), calls=%async_computation.4 | async-start | bytes 163840 | tf_op jit(solution)/shard_map/while/body/eval_jaxpr/reduce_scatter | solution.py:129
  595.4 4.2 copy-start.3
  595.4 4.2 copy-start.5
  602.2 1.4 copy-start
  605.8 72.6 %reduce-scatter.4.cloned.1.call-start = ((), (), s32[]{:S(2)}) async-start(), calls=%async_computation.3 | async-start | bytes 1179648 | tf_op jit(solution)/shard_map/while/body/eval_jaxpr/reduce_scatter | solution.py:127
Sparse Core Ops, SparseCore 0:
  121.8 21.4 reduce-scatter.7
  146.0 23.8 reduce-scatter.5
  172.2 32.2 reduce-scatter.3
  278.9 22.4 reduce-scatter.7
  304.0 23.8 reduce-scatter.5
  330.0 32.4 reduce-scatter.3
  436.8 22.3 reduce-scatter.7
  461.9 23.8 reduce-scatter.5
  488.0 32.4 reduce-scatter.3
  594.8 22.2 reduce-scatter.7
  619.9 23.8 reduce-scatter.5
  645.9 32.4 reduce-scatter.3
where the time goes:
time: 694 us; the launch traced here: 692 us
  waiting for transfers between devices  264 us (38%)
  blocking collectives  260 us (37%)
  matrix products  80.2 us (12%)
  local copies, waits for them, and re-layouts  51.5 us (7%)
  between operations  14.1 us (2%)
  other arithmetic  12.6 us (2%)
  loops' own time  9.26 us (1%)
    reduce_scatter x4, waiting for transfers between devices, group_step(): lax.psum_scatter(query_total, 'qrow', scatter_dimension=0, tiled=True)  133 us
    all_gather x8, blocking collectives, merged_2(): everything = jax.tree.map(lambda part: lax.all_gather(part, axis), array)  112 us
    reduce_scatter x4, waiting for transfers between devices, group_step(): lax.psum_scatter(key_total, 'kcol', scatter_dimension=0, tiled=True)  101 us
    all_gather x4, blocking collectives, group_step(): lax.all_gather(grad_cols, 'qrow', axis=0, tiled=True)  57 us
    all_gather x4, blocking collectives, group_step(): lax.all_gather(query_cols, 'qrow', axis=0, tiled=True)  56.3 us
    reduce_scatter x4, waiting for transfers between devices, group_step(): lax.psum_scatter(value_total, 'kcol', scatter_dimension=0, tiled=True)  30 us
    dot_general x8, matrix products, group_step(): jnp.einsum('qhd,kd->hqk', pair_grad, value_head, preferred_element_type=j...  26.8 us
    dot_general x8, matrix products, group_step(): jnp.einsum('hqk,qhd->kd', weights.astype(jnp.bfloat16), pair_grad, prefer...  22.3 us
  transfers between devices with their start and end apart: 12, of which 12 were waited for; matrix products, arithmetic and copies ran while one was open for 9% of the time, Pallas kernels for 0%

commit v1 on v0

v1 whole, which is shorter than its diff:
```python
import functools
import math

import jax
import jax.numpy as jnp
from jax import lax
from jax.experimental import pallas as pl
from jax.experimental.pallas import tpu as pltpu
from jax.sharding import PartitionSpec as P

HEADS = 16
KV_HEADS = 4
HEAD = 64
STRETCH = 64
MEMBERS = HEADS // KV_HEADS
LANES = MEMBERS * STRETCH
KB = 512


def attention_kernel(
    key_at, query_at, q_ref, g_ref, o_ref, kv_ref, dq_ref, dkv_ref,
    kvs, kts, scr, acc, xq_t, xg_t, xq, xg,
):
    tokens = kv_ref.shape[0]
    stretches = tokens // STRETCH
    f32, bf16 = jnp.float32, jnp.bfloat16
    lane = lax.broadcasted_iota(jnp.int32, (1, 2 * HEAD), 1)
    scale = jnp.where(lane < HEAD, 0.125, 1.0).astype(f32)

    def place(t, c):
        src = pl.multiple_of(t * STRETCH, STRETCH)
        dst = pl.multiple_of(key_at[t] * STRETCH, STRETCH)
        kvs[pl.ds(dst, STRETCH), :] = (kv_ref[pl.ds(src, STRETCH), :].astype(f32) * scale).astype(bf16)
        return c

    lax.fori_loop(0, stretches, place, 0)

    def turn(j, c):
        rows = pl.multiple_of(j * KB, KB)
        kts[j] = jnp.transpose(kvs[pl.ds(rows, KB), :])[HEAD:, :]
        acc[pl.ds(rows, KB), :] = jnp.zeros((KB, 2 * HEAD), f32)
        return c

    lax.fori_loop(0, tokens // KB, turn, 0)

    def by_head(block):
        flat = jnp.transpose(block.astype(f32))
        return jnp.concatenate([flat[h * HEAD : (h + 1) * HEAD] for h in range(MEMBERS)], axis=1)

    def one_stretch(st, c):
        rows = pl.multiple_of(st * STRETCH, STRETCH)
        at = query_at[st]
        q_t = by_head(q_ref[pl.ds(rows, STRETCH), :]) * 0.125
        g_t = by_head(g_ref[pl.ds(rows, STRETCH), :])
        o_t = by_head(o_ref[pl.ds(rows, STRETCH), :])
        delta = jnp.sum(g_t * o_t, axis=0, keepdims=True) * 0.125
        zero_t = jnp.zeros((HEAD, LANES), f32)
        q_pad = jnp.concatenate([zero_t, q_t], axis=0)
        g_pad = jnp.concatenate([g_t, zero_t], axis=0)
        xq_t[...] = q_pad.astype(bf16)
        xg_t[...] = g_pad.astype(bf16)
        xq[...] = jnp.transpose(q_pad).astype(bf16)
        xg[...] = jnp.transpose(g_pad).astype(bf16)
        full = (at * STRETCH) // KB

        def scores(j):
            kr = pl.multiple_of(j * KB, KB)
            return kr, jnp.dot(kvs[pl.ds(kr, KB), :], xq_t[...], preferred_element_type=f32)

        def fold_max(s, m):
            return jnp.maximum(m, jnp.max(s.reshape(KB // 8, 8, LANES), axis=0))

        def first(j, m):
            kr, s = scores(j)
            scr[pl.ds(kr, KB), :] = s
            return fold_max(s, m)

        m = lax.fori_loop(0, full, first, jnp.full((8, LANES), -1e30, f32))
        kr, s = scores(full)
        key_pos = kr + lax.broadcasted_iota(jnp.int32, (KB, LANES), 0)
        row_pos = at * STRETCH + lax.rem(lax.broadcasted_iota(jnp.int32, (KB, LANES), 1), STRETCH)
        s = jnp.where(key_pos <= row_pos, s, -1e30)
        scr[pl.ds(kr, KB), :] = s
        m = jnp.max(fold_max(s, m), axis=0, keepdims=True)

        def second(j, total):
            kr = pl.multiple_of(j * KB, KB)
            e = jnp.exp(scr[pl.ds(kr, KB), :] - m)
            scr[pl.ds(kr, KB), :] = e
            return total + jnp.sum(e.reshape(KB // 8, 8, LANES), axis=0)

        total = lax.fori_loop(0, full + 1, second, jnp.zeros((8, LANES), f32))
        inverse = 1.0 / jnp.sum(total, axis=0, keepdims=True)

        def third(j, dq):
            kr = pl.multiple_of(j * KB, KB)
            w = scr[pl.ds(kr, KB), :] * inverse
            dw = jnp.dot(kvs[pl.ds(kr, KB), :], xg_t[...], preferred_element_type=f32)
            ds = (w * (dw - delta)).astype(bf16)
            acc[pl.ds(kr, KB), :] += jnp.dot(
                w.astype(bf16), xg[...], preferred_element_type=f32
            ) + jnp.dot(ds, xq[...], preferred_element_type=f32)
            return dq + jnp.dot(kts[j], ds, preferred_element_type=f32)

        dq = lax.fori_loop(0, full + 1, third, jnp.zeros((HEAD, LANES), f32))
        flat = jnp.concatenate([dq[:, h * STRETCH : (h + 1) * STRETCH] for h in range(MEMBERS)], axis=0)
        dq_ref[pl.ds(rows, STRETCH), :] = jnp.transpose(flat).astype(bf16)
        return c

    lax.fori_loop(0, q_ref.shape[0] // STRETCH, one_stretch, 0)
    gain = jnp.where(lane < HEAD, 1.0, 8.0).astype(f32)

    def restore(t, c):
        dst = pl.multiple_of(t * STRETCH, STRETCH)
        src = pl.multiple_of(key_at[t] * STRETCH, STRETCH)
        dkv_ref[pl.ds(dst, STRETCH), :] = (acc[pl.ds(src, STRETCH), :] * gain).astype(dkv_ref.dtype)
        return c

    lax.fori_loop(0, stretches, restore, 0)


def attention(key_at, query_at, q, g, o, kv, out_type):
    tokens = kv.shape[0]
    vmem = pl.BlockSpec(memory_space=pltpu.VMEM)
    smem = pl.BlockSpec(memory_space=pltpu.SMEM)
    return pl.pallas_call(
        attention_kernel,
        out_shape=(
            jax.ShapeDtypeStruct(q.shape, jnp.bfloat16),
            jax.ShapeDtypeStruct((tokens, 2 * HEAD), out_type),
        ),
        in_specs=[smem, smem, vmem, vmem, vmem, vmem],
        out_specs=(vmem, vmem),
        scratch_shapes=[
            pltpu.VMEM((tokens, 2 * HEAD), jnp.bfloat16),
            pltpu.VMEM((tokens // KB, HEAD, KB), jnp.bfloat16),
            pltpu.VMEM((tokens, LANES), jnp.float32),
            pltpu.VMEM((tokens, 2 * HEAD), jnp.float32),
            pltpu.VMEM((2 * HEAD, LANES), jnp.bfloat16),
            pltpu.VMEM((2 * HEAD, LANES), jnp.bfloat16),
            pltpu.VMEM((LANES, 2 * HEAD), jnp.bfloat16),
            pltpu.VMEM((LANES, 2 * HEAD), jnp.bfloat16),
        ],
        compiler_params=pltpu.CompilerParams(vmem_limit_bytes=52 * 1024 * 1024),
    )(key_at, query_at, q, g, o, kv)


def per_device(queries, keys, values, outputs, out_grad, positions):
    rows = queries.shape[0]
    ranks = lax.axis_size("qrow")
    cols = lax.axis_size("kcol")
    halves = cols // KV_HEADS
    part = rows // halves
    mine = lax.axis_index("qrow")
    half = lax.rem(lax.axis_index("kcol"), halves)
    key_at = positions.reshape(-1, STRETCH)[:, 0] // STRETCH
    query_at = lax.dynamic_slice(
        key_at.reshape(cols, ranks, halves, part // STRETCH),
        (0, mine, half, 0),
        (cols, 1, 1, part // STRETCH),
    ).reshape(-1)

    def by_query(x):
        x = x.reshape(halves, part, KV_HEADS, LANES).transpose(2, 0, 1, 3)
        x = lax.all_to_all(x.reshape(cols, part, LANES), "kcol", 0, 0)
        return x.reshape(cols * part, LANES)

    def by_key(x):
        x = x.reshape(rows, KV_HEADS, 1, HEAD).transpose(1, 2, 0, 3)
        x = jnp.broadcast_to(x, (KV_HEADS, halves, rows, HEAD)).reshape(cols, rows, HEAD)
        return lax.all_to_all(x, "kcol", 0, 0).reshape(cols * rows, HEAD)

    q, g, o = by_query(queries), by_query(out_grad), by_query(outputs)
    own = jnp.concatenate([by_key(values), by_key(keys)], axis=1)
    kv = lax.all_gather(own, "qrow", axis=0, tiled=True)
    dq, dkv = attention(key_at, query_at, q, g, o, kv, jnp.float32)
    dq = lax.all_to_all(dq.reshape(cols, part, LANES), "kcol", 0, 0)
    query_grad = (
        dq.reshape(KV_HEADS, halves, part, LANES).transpose(1, 2, 0, 3).reshape(rows, HEADS * HEAD)
    )
    share = lax.psum_scatter(dkv, "qrow", scatter_dimension=0, tiled=True)
    if halves == 1:
        share = share.astype(jnp.bfloat16)

    def home(x):
        x = lax.all_to_all(x.reshape(cols, rows, HEAD), "kcol", 0, 0)
        x = x.reshape(KV_HEADS, halves, rows, HEAD).sum(1).astype(jnp.bfloat16)
        return x.transpose(1, 0, 2).reshape(rows, KV_HEADS * HEAD)

    return (query_grad, home(share[:, HEAD:]), home(share[:, :HEAD]))


def solution(mesh):
    in_specs = (
        P(("kcol", "qrow"), None),
        P(("qrow", "kcol"), None),
        P(("qrow", "kcol"), None),
        P(("kcol", "qrow"), None),
        P(("kcol", "qrow"), None),
        P(),
    )
    out_specs = (P(("kcol", "qrow"), None), P(("qrow", "kcol"), None), P(("qrow", "kcol"), None))
    return jax.shard_map(
        per_device, mesh=mesh, in_specs=in_specs, out_specs=out_specs, check_vma=False
    )
```

time: 694 us -> 158 us (0.23)
  blocking collectives: 260 us -> 0 us
  waiting for transfers between devices: 264 us -> 67.5 us
  matrix products: 80.2 us -> 0 us
  local copies, waits for them, and re-layouts: 51.5 us -> 11.5 us
  Pallas kernels: 0 us -> 33.9 us
  starting transfers between devices: 0.38 us -> 29.1 us
  other arithmetic: 12.6 us -> 1.78 us
  loops' own time: 9.26 us -> 0 us
    all_gather x19 -> x0, blocking collectives: 260 us -> none  [the longest x8 112 us: merged_2(): everything = jax.tree.map(lambda part: lax.all_gather(part, axis), array)]
    reduce_scatter x12 -> x1, waiting for transfers between devices: 264 us -> 38.7 us  [per_device(): share = lax.psum_scatter(dkv, 'qrow', scatter_dimension=0, tiled=True)]
    dot_general x40 -> x0, matrix products: 80.2 us -> none  [the longest x8 26.8 us: group_step(): jnp.einsum('qhd,kd->hqk', pair_grad, value_head, preferred_element_type=j...]
    pallas_call x0 -> x1, Pallas kernels: none -> 33.9 us  [attention(): pl.pallas_call(attention_kernel, out_shape=(jax.ShapeDtypeStruct(q.shape,...]
    all_to_all x0 -> x8, starting transfers between devices: none -> 29 us  [the longest x3 10.2 us: by_query(): x = lax.all_to_all(x.reshape(cols, part, LANES), 'kcol', 0, 0)]
    all_to_all x0 -> x8, waiting for transfers between devices: none -> 28.8 us  [the longest x3 13.6 us: by_query(): x = lax.all_to_all(x.reshape(cols, part, LANES), 'kcol', 0, 0)]
    dynamic_update_slice x12 -> x0, local copies, waits for them, and re-layouts: 17 us -> none  [per_device(): lax.scan(group_step, jnp.zeros((), jnp.float32), jnp.arange(KV_HEADS, dty...]
    while x56 -> x0, local copies, waits for them, and re-layouts: 13.1 us -> none
  transfers between devices with their start and end apart: 12 -> 10, of which waited for: 12 -> 8; matrix products, arithmetic and copies ran while one was open for 9% -> 6% of each run, Pallas kernels for 0% -> 0%
where the time goes in v1:
time: 158 us
  waiting for transfers between devices  67.5 us (43%)
  Pallas kernels  33.9 us (21%)
  starting transfers between devices  29.1 us (18%)
  between operations  14.2 us (9%)
  local copies, waits for them, and re-layouts  11.5 us (7%)
  other arithmetic  1.78 us (1%)
    reduce_scatter x1, waiting for transfers between devices, per_device(): share = lax.psum_scatter(dkv, 'qrow', scatter_dimension=0, tiled=True)  38.7 us
    pallas_call x1, Pallas kernels, attention(): pl.pallas_call(attention_kernel, out_shape=(jax.ShapeDtypeStruct(q.shape,...  33.9 us
    all_to_all x3, waiting for transfers between devices, by_query(): x = lax.all_to_all(x.reshape(cols, part, LANES), 'kcol', 0, 0)  13.6 us
    all_to_all x3, starting transfers between devices, by_query(): x = lax.all_to_all(x.reshape(cols, part, LANES), 'kcol', 0, 0)  10.2 us
    all_to_all x2, starting transfers between devices, by_key(): return lax.all_to_all(x, 'kcol', 0, 0).reshape(cols * rows, HEAD)  8.45 us
    all_to_all x2, waiting for transfers between devices, by_key(): return lax.all_to_all(x, 'kcol', 0, 0).reshape(cols * rows, HEAD)  7.89 us
    all_to_all x2, waiting for transfers between devices, home(): x = lax.all_to_all(x.reshape(cols, rows, HEAD), 'kcol', 0, 0)  7.23 us
    all_to_all x2, starting transfers between devices, home(): x = lax.all_to_all(x.reshape(cols, rows, HEAD), 'kcol', 0, 0)  6.95 us
  transfers between devices with their start and end apart: 10, of which 8 were waited for; matrix products, arithmetic and copies ran while one was open for 6% of the time, Pallas kernels for 0%

profile of v1, /device:TPU:0, one launch (start us, length us, event | category | flops | bytes accessed | tf_op | source)
XLA Modules:
  0.0 158.0 jit_solution(15197216433004644891)
XLA Ops:
  7.2 0.0 copy-start.2
  7.2 0.0 copy-start
  7.2 1.6 %copy.34 = bf16[128,256]{0,1:T(8,128)(2,1)} copy(bf16[128,256]{1,0:T(8,128)(2,1)} %param.7) | data formatting | bytes 131072 | tf_op args[1]
  8.8 5.2 %all-to-all-start.4 = ((bf16[4,128,64]{1,2,0:T(8,128)(2,1)}), bf16[4,128,64]{1,2,0:T(8,128)(2,1)S(1)}, u32[]{:S(2)}, u32[]{:S(2)}) async-start(bf16[4,128,64]{1,2,0:T(8,128)(2,1)} %bitcast.15), calls=%async_computation.4 | async-start | bytes 131072 | tf_op jit(solution)/shard_map/all_to_all | solution.py:171
  14.0 1.6 copy.32
  15.5 3.3 %all-to-all-done.4 = bf16[4,128,64]{1,2,0:T(8,128)(2,1)S(1)} async-done(((bf16[4,128,64]{1,2,0:T(8,128)(2,1)}), bf16[4,128,64]{1,2,0:T(8,128)(2,1)S(1)}, u32[]{:S(2)}, u32[]{:S(2)}) %all-to-all-start.4) | async-done | bytes 65568 | tf_op jit(solution)/shard_map/all_to_all | solution.py:171
  18.8 3.3 %all-to-all-start.3 = ((bf16[4,128,64]{1,2,0:T(8,128)(2,1)}), bf16[4,128,64]{1,2,0:T(8,128)(2,1)S(1)}, u32[]{:S(2)}, u32[]{:S(2)}) async-start(bf16[4,128,64]{1,2,0:T(8,128)(2,1)} %bitcast.11), calls=%async_computation.3 | async-start | bytes 131072 | tf_op jit(solution)/shard_map/all_to_all | solution.py:171
  22.1 0.0 copy-start.1
  22.1 0.0 all-gather.2.cloned.1.call-start
  22.2 0.1 copy.35
  22.3 4.6 %all-to-all-done.3 = bf16[4,128,64]{1,2,0:T(8,128)(2,1)S(1)} async-done(((bf16[4,128,64]{1,2,0:T(8,128)(2,1)}), bf16[4,128,64]{1,2,0:T(8,128)(2,1)S(1)}, u32[]{:S(2)}, u32[]{:S(2)}) %all-to-all-start.3) | async-done | bytes 65568 | tf_op jit(solution)/shard_map/all_to_all | solution.py:171
  26.9 0.1 copy.33
  27.0 0.8 pad_maximum_fusion
  27.8 0.0 all-gather.2.cloned.1.call-update
  27.8 1.1 reshape.159
  29.0 0.7 copy.47
  29.7 3.4 %all-to-all-start = ((bf16[4,128,256]{2,1,0:T(8,128)(2,1)}), bf16[4,128,256]{2,1,0:T(8,128)(2,1)S(1)}, u32[]{:S(2)}, u32[]{:S(2)}) async-start(bf16[4,128,256]{2,1,0:T(8,128)(2,1)} %bitcast.44), calls=%async_computation | async-start | bytes 524288 | tf_op jit(solution)/shard_map/all_to_all | solution.py:165
  33.1 0.0 copy-done.2
  33.1 0.1 reshape.157
  33.2 0.1 slice_reduce_fusion
  33.3 0.1 squeeze.6
  33.4 0.0 copy-done
  33.4 0.2 reshape.165
  33.6 0.7 copy.45
  34.4 4.1 %all-to-all-done = bf16[4,128,256]{2,1,0:T(8,128)(2,1)S(1)} async-done(((bf16[4,128,256]{2,1,0:T(8,128)(2,1)}), bf16[4,128,256]{2,1,0:T(8,128)(2,1)S(1)}, u32[]{:S(2)}, u32[]{:S(2)}) %all-to-all-start) | async-done | bytes 262176 | tf_op jit(solution)/shard_map/all_to_all | solution.py:165
  38.5 3.4 %all-to-all-start.2 = ((bf16[4,128,256]{2,1,0:T(8,128)(2,1)}), bf16[4,128,256]{2,1,0:T(8,128)(2,1)S(1)}, u32[]{:S(2)}, u32[]{:S(2)}) async-start(bf16[4,128,256]{2,1,0:T(8,128)(2,1)} %bitcast.42), calls=%async_computation.2 | async-start | bytes 524288 | tf_op jit(solution)/shard_map/all_to_all | solution.py:165
  41.9 0.1 reshape.158.query_at
  42.0 0.0 copy-done.1
  42.0 0.2 reshape.162
  42.2 0.7 copy.46
  42.9 4.3 %all-to-all-done.2 = bf16[4,128,256]{2,1,0:T(8,128)(2,1)S(1)} async-done(((bf16[4,128,256]{2,1,0:T(8,128)(2,1)}), bf16[4,128,256]{2,1,0:T(8,128)(2,1)S(1)}, u32[]{:S(2)}, u32[]{:S(2)}) %all-to-all-start.2) | async-done | bytes 262176 | tf_op jit(solution)/shard_map/all_to_all | solution.py:165
  47.2 3.4 %all-to-all-start.1 = ((bf16[4,128,256]{2,1,0:T(8,128)(2,1)}), bf16[4,128,256]{2,1,0:T(8,128)(2,1)S(1)}, u32[]{:S(2)}, u32[]{:S(2)}) async-start(bf16[4,128,256]{2,1,0:T(8,128)(2,1)} %bitcast.43), calls=%async_computation.1 | async-start | bytes 524288 | tf_op jit(solution)/shard_map/all_to_all | solution.py:165
  50.6 0.0 reduce-scatter.2.cloned.1.call-start
  50.7 5.3 %all-to-all-done.1 = bf16[4,128,256]{2,1,0:T(8,128)(2,1)S(1)} async-done(((bf16[4,128,256]{2,1,0:T(8,128)(2,1)}), bf16[4,128,256]{2,1,0:T(8,128)(2,1)S(1)}, u32[]{:S(2)}, u32[]{:S(2)}) %all-to-all-start.1) | async-done | bytes 262176 | tf_op jit(solution)/shard_map/all_to_all | solution.py:165
  56.0 0.0 all-gather.2.cloned.1.call-done.kv_ref
  56.0 33.9 %shard_map.85 = (bf16[512,256]{1,0:T(8,128)(2,1)}, f32[4096,128]{1,0:T(8,128)}) custom-call(s32[64]{0:T(128)S(1)} %and_select_fusion.1.key_at, s32[8]{0:T(128)S(1)} %reshape.158.query_at, bf16[512,256]{1,0:T(8,128)(2,1)S(1)} %bitcast.45, bf16[512,256]{1,0:T(8,128)(2,1)S(1)} %bitcast.47, bf16[512,256]{1,0:T(8,128)(2,1)S(1)} %bitcast.46, ...), custom_call_target="tpu_custom_call" | custom-call | tf_op jit(solution)/shard_map/pallas_call | solution.py:126
  89.9 0.0 reduce-scatter.2.cloned.1.call-update
  89.9 3.4 %all-to-all-start.5 = ((bf16[4,128,256]{2,1,0:T(8,128)(2,1)}), bf16[4,128,256]{2,1,0:T(8,128)(2,1)S(1)}, u32[]{:S(2)}, u32[]{:S(2)}) async-start(bf16[4,128,256]{2,1,0:T(8,128)(2,1)} %bitcast.17), calls=%async_computation.5 | async-start | bytes 524288 | tf_op jit(solution)/shard_map/all_to_all | solution.py:177
  93.4 38.7 %reduce-scatter.2.cloned.1.call-done = f32[512,128]{1,0:T(8,128)} async-done(((f32[4096,128]{1,0:T(8,128)}), f32[512,128]{1,0:T(8,128)}) %reduce-scatter.2.cloned.1.call-update) | async-done | bytes 262160 | tf_op jit(solution)/shard_map/reduce_scatter | solution.py:181
  132.0 1.0 convert_element_type.4
  133.0 0.1 fusion.1
  133.1 0.7 copy.37
  133.8 0.0 all-to-all-done.5
  133.8 3.7 %all-to-all-start.6 = ((bf16[4,128,64]{1,2,0:T(8,128)(2,1)}), bf16[4,128,64]{1,2,0:T(8,128)(2,1)S(1)}, u32[]{:S(2)}, u32[]{:S(2)}) async-start(bf16[4,128,64]{1,2,0:T(8,128)(2,1)} %copy.37), calls=%async_computation.7 | async-start | bytes 131072 | tf_op jit(solution)/shard_map/all_to_all | solution.py:186
  137.5 0.7 copy.38
  138.2 4.1 %all-to-all-done.6 = bf16[4,128,64]{1,2,0:T(8,128)(2,1)S(1)} async-done(((bf16[4,128,64]{1,2,0:T(8,128)(2,1)}), bf16[4,128,64]{1,2,0:T(8,128)(2,1)S(1)}, u32[]{:S(2)}, u32[]{:S(2)}) %all-to-all-start.6) | async-done | bytes 65568 | tf_op jit(solution)/shard_map/all_to_all | solution.py:186
  142.3 3.3 %all-to-all-start.7 = ((bf16[4,128,64]{1,2,0:T(8,128)(2,1)}), bf16[4,128,64]{1,2,0:T(8,128)(2,1)S(1)}, u32[]{:S(2)}, u32[]{:S(2)}) async-start(bf16[4,128,64]{1,2,0:T(8,128)(2,1)} %copy.38), calls=%async_computation.8 | async-start | bytes 131072 | tf_op jit(solution)/shard_map/all_to_all | solution.py:186
  145.6 0.2 copy.36
  145.9 0.7 copy.41
  146.6 0.7 copy.39
  147.3 3.1 %all-to-all-done.7 = bf16[4,128,64]{1,2,0:T(8,128)(2,1)S(1)} async-done(((bf16[4,128,64]{1,2,0:T(8,128)(2,1)}), bf16[4,128,64]{1,2,0:T(8,128)(2,1)S(1)}, u32[]{:S(2)}, u32[]{:S(2)}) %all-to-all-start.7) | async-done | bytes 65568 | tf_op jit(solution)/shard_map/all_to_all | solution.py:186
  150.5 0.7 copy.40
  (4 shorter events, 0.1 us)
Async XLA Ops:
  7.2 26.0 %copy-start.2 = (s32[4096]{0:T(1024)S(1)}, s32[4096]{0:T(1024)}, u32[]{:S(2)}) copy-start(s32[4096]{0:T(1024)} %param.11) | copy-start | bytes 49156
  7.2 26.3 %copy-start = (bf16[128,1024]{1,0:T(8,128)(2,1)S(1)}, bf16[128,1024]{1,0:T(8,128)(2,1)}, u32[]{:S(2)}) copy-start(bf16[128,1024]{1,0:T(8,128)(2,1)} %param.9) | copy-start | bytes 786436
  8.8 10.0 %all-to-all-start.4 = ((bf16[4,128,64]{1,2,0:T(8,128)(2,1)}), bf16[4,128,64]{1,2,0:T(8,128)(2,1)S(1)}, u32[]{:S(2)}, u32[]{:S(2)}) async-start(bf16[4,128,64]{1,2,0:T(8,128)(2,1)} %bitcast.15), calls=%async_computation.4 | async-start | bytes 131072 | tf_op jit(solution)/shard_map/all_to_all | solution.py:171
  18.8 8.1 %all-to-all-start.3 = ((bf16[4,128,64]{1,2,0:T(8,128)(2,1)}), bf16[4,128,64]{1,2,0:T(8,128)(2,1)S(1)}, u32[]{:S(2)}, u32[]{:S(2)}) async-start(bf16[4,128,64]{1,2,0:T(8,128)(2,1)} %bitcast.11), calls=%async_computation.3 | async-start | bytes 131072 | tf_op jit(solution)/shard_map/all_to_all | solution.py:171
  22.1 19.9 %copy-start.1 = (bf16[128,1024]{1,0:T(8,128)(2,1)S(1)}, bf16[128,1024]{1,0:T(8,128)(2,1)}, u32[]{:S(2)}) copy-start(bf16[128,1024]{1,0:T(8,128)(2,1)} %param.10) | copy-start | bytes 786436
  22.1 33.9 %all-gather.2.cloned.1.call-start = ((), (), s32[]{:S(2)}) async-start(), calls=%async_computation.9 | async-start | bytes 1179648 | tf_op jit(solution)/shard_map/all_gather | solution.py:175
  29.7 8.8 %all-to-all-start = ((bf16[4,128,256]{2,1,0:T(8,128)(2,1)}), bf16[4,128,256]{2,1,0:T(8,128)(2,1)S(1)}, u32[]{:S(2)}, u32[]{:S(2)}) async-start(bf16[4,128,256]{2,1,0:T(8,128)(2,1)} %bitcast.44), calls=%async_computation | async-start | bytes 524288 | tf_op jit(solution)/shard_map/all_to_all | solution.py:165
  38.5 8.8 %all-to-all-start.2 = ((bf16[4,128,256]{2,1,0:T(8,128)(2,1)}), bf16[4,128,256]{2,1,0:T(8,128)(2,1)S(1)}, u32[]{:S(2)}, u32[]{:S(2)}) async-start(bf16[4,128,256]{2,1,0:T(8,128)(2,1)} %bitcast.42), calls=%async_computation.2 | async-start | bytes 524288 | tf_op jit(solution)/shard_map/all_to_all | solution.py:165
  47.2 8.8 %all-to-all-start.1 = ((bf16[4,128,256]{2,1,0:T(8,128)(2,1)}), bf16[4,128,256]{2,1,0:T(8,128)(2,1)S(1)}, u32[]{:S(2)}, u32[]{:S(2)}) async-start(bf16[4,128,256]{2,1,0:T(8,128)(2,1)} %bitcast.43), calls=%async_computation.1 | async-start | bytes 524288 | tf_op jit(solution)/shard_map/all_to_all | solution.py:165
  50.6 81.4 %reduce-scatter.2.cloned.1.call-start = ((), (), s32[]{:S(2)}) async-start(), calls=%async_computation.10 | async-start | bytes 2359296 | tf_op jit(solution)/shard_map/reduce_scatter | solution.py:181
  89.9 43.9 %all-to-all-start.5 = ((bf16[4,128,256]{2,1,0:T(8,128)(2,1)}), bf16[4,128,256]{2,1,0:T(8,128)(2,1)S(1)}, u32[]{:S(2)}, u32[]{:S(2)}) async-start(bf16[4,128,256]{2,1,0:T(8,128)(2,1)} %bitcast.17), calls=%async_computation.5 | async-start | bytes 524288 | tf_op jit(solution)/shard_map/all_to_all | solution.py:177
  133.8 8.5 %all-to-all-start.6 = ((bf16[4,128,64]{1,2,0:T(8,128)(2,1)}), bf16[4,128,64]{1,2,0:T(8,128)(2,1)S(1)}, u32[]{:S(2)}, u32[]{:S(2)}) async-start(bf16[4,128,64]{1,2,0:T(8,128)(2,1)} %copy.37), calls=%async_computation.7 | async-start | bytes 131072 | tf_op jit(solution)/shard_map/all_to_all | solution.py:186
  142.3 8.1 %all-to-all-start.7 = ((bf16[4,128,64]{1,2,0:T(8,128)(2,1)}), bf16[4,128,64]{1,2,0:T(8,128)(2,1)S(1)}, u32[]{:S(2)}, u32[]{:S(2)}) async-start(bf16[4,128,64]{1,2,0:T(8,128)(2,1)} %copy.38), calls=%async_computation.8 | async-start | bytes 131072 | tf_op jit(solution)/shard_map/all_to_all | solution.py:186
Sparse Core Ops, SparseCore 0:
  28.0 21.6 all-gather.1
  90.1 41.9 reduce-scatter.1

commit v2 on v1

--- a/solution.py
+++ b/solution.py
@@ -1,5 +1,4 @@
 import functools
-import math
 
 import jax
 import jax.numpy as jnp
@@ -18,19 +17,19 @@
 
 
 def attention_kernel(
-    key_at, query_at, q_ref, g_ref, o_ref, kv_ref, dq_ref, dkv_ref,
+    key_at, query_at, q_ref, g_ref, d_ref, kv_ref, dq_ref, dkv_ref,
     kvs, kts, scr, acc, xq_t, xg_t, xq, xg,
 ):
     tokens = kv_ref.shape[0]
     stretches = tokens // STRETCH
     f32, bf16 = jnp.float32, jnp.bfloat16
     lane = lax.broadcasted_iota(jnp.int32, (1, 2 * HEAD), 1)
-    scale = jnp.where(lane < HEAD, 0.125, 1.0).astype(f32)
+    each = q_ref.shape[0] // STRETCH // d_ref.shape[0]
 
     def place(t, c):
         src = pl.multiple_of(t * STRETCH, STRETCH)
         dst = pl.multiple_of(key_at[t] * STRETCH, STRETCH)
-        kvs[pl.ds(dst, STRETCH), :] = (kv_ref[pl.ds(src, STRETCH), :].astype(f32) * scale).astype(bf16)
+        kvs[pl.ds(dst, STRETCH), :] = kv_ref[pl.ds(src, STRETCH), :]
         return c
 
     lax.fori_loop(0, stretches, place, 0)
@@ -52,8 +51,7 @@
         at = query_at[st]
         q_t = by_head(q_ref[pl.ds(rows, STRETCH), :]) * 0.125
         g_t = by_head(g_ref[pl.ds(rows, STRETCH), :])
-        o_t = by_head(o_ref[pl.ds(rows, STRETCH), :])
-        delta = jnp.sum(g_t * o_t, axis=0, keepdims=True) * 0.125
+        delta = d_ref[st // each, pl.ds(lax.rem(st, each), 1), :]
         zero_t = jnp.zeros((HEAD, LANES), f32)
         q_pad = jnp.concatenate([zero_t, q_t], axis=0)
         g_pad = jnp.concatenate([g_t, zero_t], axis=0)
@@ -119,7 +117,7 @@
     lax.fori_loop(0, stretches, restore, 0)
 
 
-def attention(key_at, query_at, q, g, o, kv, out_type):
+def attention(key_at, query_at, q, g, d, kv, out_type):
     tokens = kv.shape[0]
     vmem = pl.BlockSpec(memory_space=pltpu.VMEM)
     smem = pl.BlockSpec(memory_space=pltpu.SMEM)
@@ -142,7 +140,290 @@
             pltpu.VMEM((LANES, 2 * HEAD), jnp.bfloat16),
         ],
         compiler_params=pltpu.CompilerParams(vmem_limit_bytes=52 * 1024 * 1024),
-    )(key_at, query_at, q, g, o, kv)
+    )(key_at, query_at, q, g, d, kv)
+
+
+def greet(ranks, cols):
+    r, c = lax.axis_index("qrow"), lax.axis_index("kcol")
+    barrier = pltpu.get_barrier_semaphore()
+    count = 0
+    for k in range(1, cols):
+        signal(barrier, (r, lax.rem(c + k, cols)))
+        count += 1
+    for k in range(1, ranks // 2):
+        signal(barrier, (lax.rem(r + 2 * k, ranks), c))
+        count += 1
+    signal(barrier, (r + 1 - 2 * lax.rem(r, 2), c))
+    pl.semaphore_wait(barrier, count + 1)
+
+
+def signal(semaphore, device):
+    pl.semaphore_signal(
+        semaphore, inc=1, device_id=device, device_id_type=pl.DeviceIdType.MESH
+    )
+
+
+def remote(src, dst, send, recv, device):
+    return pltpu.make_async_remote_copy(
+        src_ref=src, dst_ref=dst, send_sem=send, recv_sem=recv,
+        device_id=device, device_id_type=pl.DeviceIdType.MESH,
+    )
+
+
+def gather_kernel(
+    ranks, cols, q_ref, g_ref, o_ref, k_ref, v_ref, q_out, g_out, d_out, kv_out,
+    packed, terms, send_a, recv_a, send_z, recv_z, send_s, recv_s,
+):
+    f32, bf16 = jnp.float32, jnp.bfloat16
+    r, c = lax.axis_index("qrow"), lax.axis_index("kcol")
+    sibling = r + 1 - 2 * lax.rem(r, 2)
+    rows = q_ref.shape[0]
+    halves = cols // KV_HEADS
+    part = rows // halves
+    block = cols * rows
+    greet(ranks, cols)
+
+    def key_rows(rank, col):
+        return pl.ds(pl.multiple_of((rank * cols + col) * rows, rows), rows)
+
+    def query_rows(col):
+        return pl.ds(pl.multiple_of(col * part, part), part)
+
+    def query_slice(col):
+        half = pl.ds(pl.multiple_of(lax.rem(col, halves) * part, part), part)
+        return half, pl.ds(pl.multiple_of((col // halves) * LANES, LANES), LANES)
+
+    for h in range(KV_HEADS):
+        cut = slice(h * HEAD, (h + 1) * HEAD)
+        packed[h] = jnp.concatenate(
+            [(v_ref[:, cut].astype(f32) * 0.125).astype(bf16), k_ref[:, cut]], axis=1
+        )
+
+    def to_peer(k, which, src, dst, peer):
+        return remote(src, dst, send_a.at[k, which], recv_a.at[k, which], (r, peer))
+
+    copies = []
+    for k in range(1, cols):
+        peer = lax.rem(c + k, cols)
+        copies.append(
+            to_peer(k, 0, packed.at[peer // halves], kv_out.at[key_rows(r, c)], peer)
+        )
+        copies[-1].start()
+    for k in range(1, cols):
+        peer = lax.rem(c + k, cols)
+        for which, (src, dst) in enumerate([(q_ref, q_out), (g_ref, g_out)]):
+            half, columns = query_slice(peer)
+            copies.append(
+                to_peer(k, 1 + which, src.at[half, columns], dst.at[query_rows(c)], peer)
+            )
+            copies[-1].start()
+    kv_out[key_rows(r, c), :] = packed[c // halves]
+    half, columns = query_slice(c)
+    q_out[query_rows(c), :] = q_ref[half, columns]
+    g_out[query_rows(c), :] = g_ref[half, columns]
+
+    for h in range(KV_HEADS):
+        cut = slice(h * LANES, (h + 1) * LANES)
+        product = jnp.transpose(g_ref[:, cut].astype(f32) * o_ref[:, cut].astype(f32))
+        sums = jnp.sum(product.reshape(MEMBERS, HEAD, rows), axis=1) * 0.125
+        for u in range(rows // STRETCH):
+            line = jnp.concatenate(
+                [sums[m : m + 1, u * STRETCH : (u + 1) * STRETCH] for m in range(MEMBERS)], axis=1
+            )
+            each = part // STRETCH
+            terms[h * halves + u // each, u % each : u % each + 1, :] = line
+    for k in range(1, cols):
+        peer = lax.rem(c + k, cols)
+        copies.append(to_peer(k, 3, terms.at[peer], d_out.at[c], peer))
+        copies[-1].start()
+    d_out[c] = terms[c]
+
+    def from_peer(k, which, dst):
+        return remote(dst, dst, send_a.at[k, which], recv_a.at[k, which], (r, lax.rem(c + k, cols)))
+
+    for k in range(1, cols):
+        source = lax.rem(c + cols - k, cols)
+        from_peer(k, 0, kv_out.at[key_rows(r, source)]).wait_recv()
+
+    def whole(rank):
+        return kv_out.at[pl.ds(pl.multiple_of(rank * block, block), block)]
+
+    for k in range(1, ranks // 2):
+        peer = lax.rem(r + 2 * k, ranks)
+        copies.append(remote(whole(r), whole(r), send_z.at[k], recv_z.at[k], (peer, c)))
+        copies[-1].start()
+    copies.append(remote(whole(r), whole(r), send_s.at[0], recv_s.at[0], (sibling, c)))
+    copies[-1].start()
+    for k in range(1, ranks // 2):
+        source = lax.rem(r + ranks - 2 * k, ranks)
+        peer = lax.rem(r + 2 * k, ranks)
+        here = whole(source)
+        remote(here, here, send_z.at[k], recv_z.at[k], (peer, c)).wait_recv()
+        copies.append(remote(here, here, send_s.at[k], recv_s.at[k], (sibling, c)))
+        copies[-1].start()
+    for k in range(ranks // 2):
+        here = whole(lax.rem(sibling + ranks - 2 * k, ranks))
+        remote(here, here, send_s.at[k], recv_s.at[k], (sibling, c)).wait_recv()
+    for k in range(1, cols):
+        source = lax.rem(c + cols - k, cols)
+        from_peer(k, 1, q_out.at[query_rows(source)]).wait_recv()
+        from_peer(k, 2, g_out.at[query_rows(source)]).wait_recv()
+        from_peer(k, 3, d_out.at[source]).wait_recv()
+    for copy in copies:
+        copy.wait_send()
+
+
+def gather(queries, out_grad, outputs, keys, values, ranks, cols):
+    rows = queries.shape[0]
+    part = rows // (cols // KV_HEADS)
+    bf16 = jnp.bfloat16
+    vmem = pl.BlockSpec(memory_space=pltpu.VMEM)
+    dma = pltpu.SemaphoreType.DMA
+    return pl.pallas_call(
+        functools.partial(gather_kernel, ranks, cols),
+        out_shape=(
+            jax.ShapeDtypeStruct((cols * part, LANES), bf16),
+            jax.ShapeDtypeStruct((cols * part, LANES), bf16),
+            jax.ShapeDtypeStruct((cols, 8, LANES), jnp.float32),
+            jax.ShapeDtypeStruct((ranks * cols * rows, 2 * HEAD), bf16),
+        ),
+        in_specs=[vmem] * 5,
+        out_specs=(vmem,) * 4,
+        scratch_shapes=[
+            pltpu.VMEM((KV_HEADS, rows, 2 * HEAD), bf16),
+            pltpu.VMEM((cols, 8, LANES), jnp.float32),
+            dma((cols, 4)), dma((cols, 4)),
+            dma((ranks // 2,)), dma((ranks // 2,)),
+            dma((ranks // 2,)), dma((ranks // 2,)),
+        ],
+        compiler_params=pltpu.CompilerParams(
+            collective_id=0, has_side_effects=True, vmem_limit_bytes=40 * 1024 * 1024
+        ),
+    )(queries, out_grad, outputs, keys, values)
+
+
+def scatter_kernel(
+    ranks, cols, dq_ref, dkv_ref, q_out, k_out, v_out,
+    near, passing, far, share, last,
+    send_q, recv_q, send_s, recv_s, send_z, recv_z, send_a, recv_a,
+):
+    f32, bf16 = jnp.float32, jnp.bfloat16
+    r, c = lax.axis_index("qrow"), lax.axis_index("kcol")
+    sibling = r + 1 - 2 * lax.rem(r, 2)
+    rows = q_out.shape[0]
+    halves = cols // KV_HEADS
+    part = rows // halves
+    block = cols * rows
+    steps = ranks // 2
+    greet(ranks, cols)
+
+    def span(rank):
+        return pl.ds(pl.multiple_of(rank * block, block), block)
+
+    def query_rows(col):
+        return pl.ds(pl.multiple_of(col * part, part), part)
+
+    def query_slice(col):
+        half = pl.ds(pl.multiple_of(lax.rem(col, halves) * part, part), part)
+        return half, pl.ds(pl.multiple_of((col // halves) * LANES, LANES), LANES)
+
+    copies = []
+    order = list(range(1, steps)) + [0]
+    for k in order:
+        target = lax.rem(sibling + 2 * k, ranks)
+        copies.append(
+            remote(dkv_ref.at[span(target)], near.at[k], send_s.at[k], recv_s.at[k], (sibling, c))
+        )
+        copies[-1].start()
+    for k in order:
+        peer = lax.rem(r + 2 * k, ranks)
+        remote(near.at[k], near.at[k], send_s.at[k], recv_s.at[k], (sibling, c)).wait_recv()
+        both = dkv_ref[span(peer), :].astype(f32) + near[k].astype(f32)
+        if k:
+            passing[k] = both.astype(bf16)
+            copies.append(
+                remote(passing.at[k], far.at[k], send_z.at[k], recv_z.at[k], (peer, c))
+            )
+            copies[-1].start()
+    half, columns = query_slice(c)
+    for k in range(1, cols):
+        peer = lax.rem(c + k, cols)
+        copies.append(
+            remote(
+                dq_ref.at[query_rows(peer)], q_out.at[half, columns],
+                send_q.at[k], recv_q.at[k], (r, peer),
+            )
+        )
+        copies[-1].start()
+    q_out[half, columns] = dq_ref[query_rows(c), :]
+    total = both
+    for k in range(1, steps):
+        peer = lax.rem(r + 2 * k, ranks)
+        remote(far.at[k], far.at[k], send_z.at[k], recv_z.at[k], (peer, c)).wait_recv()
+        total = total + far[k].astype(f32)
+    share[...] = total.astype(bf16)
+
+    def share_rows(col):
+        return pl.ds(pl.multiple_of(col * rows, rows), rows)
+
+    for k in range(1, cols):
+        peer = lax.rem(c + k, cols)
+        copies.append(
+            remote(share.at[share_rows(peer)], last.at[c], send_a.at[k], recv_a.at[k], (r, peer))
+        )
+        copies[-1].start()
+    last[c] = share[share_rows(c), :]
+    for k in range(1, cols):
+        peer = lax.rem(c + k, cols)
+        here = last.at[lax.rem(c + cols - k, cols)]
+        remote(here, here, send_a.at[k], recv_a.at[k], (r, peer)).wait_recv()
+    k_parts, v_parts = [], []
+    for h in range(KV_HEADS):
+        whole = last[h * halves].astype(f32)
+        for other in range(1, halves):
+            whole = whole + last[h * halves + other].astype(f32)
+        v_parts.append(whole[:, :HEAD])
+        k_parts.append(whole[:, HEAD:])
+    k_out[...] = jnp.concatenate(k_parts, axis=1).astype(bf16)
+    v_out[...] = jnp.concatenate(v_parts, axis=1).astype(bf16)
+    for k in range(1, cols):
+        peer = lax.rem(c + k, cols)
+        half, columns = query_slice(lax.rem(c + cols - k, cols))
+        here = q_out.at[half, columns]
+        remote(dq_ref.at[query_rows(peer)], here, send_q.at[k], recv_q.at[k], (r, peer)).wait_recv()
+    for copy in copies:
+        copy.wait_send()
+
+
+def scatter(dq, dkv, rows, ranks, cols):
+    bf16 = jnp.bfloat16
+    vmem = pl.BlockSpec(memory_space=pltpu.VMEM)
+    dma = pltpu.SemaphoreType.DMA
+    block = cols * rows
+    return pl.pallas_call(
+        functools.partial(scatter_kernel, ranks, cols),
+        out_shape=(
+            jax.ShapeDtypeStruct((rows, HEADS * HEAD), bf16),
+            jax.ShapeDtypeStruct((rows, KV_HEADS * HEAD), bf16),
+            jax.ShapeDtypeStruct((rows, KV_HEADS * HEAD), bf16),
+        ),
+        in_specs=[vmem] * 2,
+        out_specs=(vmem,) * 3,
+        scratch_shapes=[
+            pltpu.VMEM((ranks // 2, block, 2 * HEAD), bf16),
+            pltpu.VMEM((ranks // 2, block, 2 * HEAD), bf16),
+            pltpu.VMEM((ranks // 2, block, 2 * HEAD), bf16),
+            pltpu.VMEM((block, 2 * HEAD), bf16),
+            pltpu.VMEM((cols, rows, 2 * HEAD), bf16),
+            dma((cols,)), dma((cols,)),
+            dma((ranks // 2,)), dma((ranks // 2,)),
+            dma((ranks // 2,)), dma((ranks // 2,)),
+            dma((cols,)), dma((cols,)),
+        ],
+        compiler_params=pltpu.CompilerParams(
+            collective_id=1, has_side_effects=True, vmem_limit_bytes=40 * 1024 * 1024
+        ),
+    )(dq, dkv)
 
 
 def per_device(queries, keys, values, outputs, out_grad, positions):
@@ -150,44 +431,16 @@
     ranks = lax.axis_size("qrow")
     cols = lax.axis_size("kcol")
     halves = cols // KV_HEADS
-    part = rows // halves
+    each = rows // halves // STRETCH
     mine = lax.axis_index("qrow")
     half = lax.rem(lax.axis_index("kcol"), halves)
     key_at = positions.reshape(-1, STRETCH)[:, 0] // STRETCH
     query_at = lax.dynamic_slice(
-        key_at.reshape(cols, ranks, halves, part // STRETCH),
-        (0, mine, half, 0),
-        (cols, 1, 1, part // STRETCH),
+        key_at.reshape(cols, ranks, halves, each), (0, mine, half, 0), (cols, 1, 1, each)
     ).reshape(-1)
-
-    def by_query(x):
-        x = x.reshape(halves, part, KV_HEADS, LANES).transpose(2, 0, 1, 3)
-        x = lax.all_to_all(x.reshape(cols, part, LANES), "kcol", 0, 0)
-        return x.reshape(cols * part, LANES)
-
-    def by_key(x):
-        x = x.reshape(rows, KV_HEADS, 1, HEAD).transpose(1, 2, 0, 3)
-        x = jnp.broadcast_to(x, (KV_HEADS, halves, rows, HEAD)).reshape(cols, rows, HEAD)
-        return lax.all_to_all(x, "kcol", 0, 0).reshape(cols * rows, HEAD)
-
-    q, g, o = by_query(queries), by_query(out_grad), by_query(outputs)
-    own = jnp.concatenate([by_key(values), by_key(keys)], axis=1)
-    kv = lax.all_gather(own, "qrow", axis=0, tiled=True)
-    dq, dkv = attention(key_at, query_at, q, g, o, kv, jnp.float32)
-    dq = lax.all_to_all(dq.reshape(cols, part, LANES), "kcol", 0, 0)
-    query_grad = (
-        dq.reshape(KV_HEADS, halves, part, LANES).transpose(1, 2, 0, 3).reshape(rows, HEADS * HEAD)
-    )
-    share = lax.psum_scatter(dkv, "qrow", scatter_dimension=0, tiled=True)
-    if halves == 1:
-        share = share.astype(jnp.bfloat16)
-
-    def home(x):
-        x = lax.all_to_all(x.reshape(cols, rows, HEAD), "kcol", 0, 0)
-        x = x.reshape(KV_HEADS, halves, rows, HEAD).sum(1).astype(jnp.bfloat16)
-        return x.transpose(1, 0, 2).reshape(rows, KV_HEADS * HEAD)
-
-    return (query_grad, home(share[:, HEAD:]), home(share[:, :HEAD]))
+    q, g, d, kv = gather(queries, out_grad, outputs, keys, values, ranks, cols)
+    dq, dkv = attention(key_at, query_at, q, g, d, kv, jnp.bfloat16)
+    return scatter(dq, dkv, rows, ranks, cols)
 
 
 def solution(mesh):

time: 158 us -> 88.2 us (0.56)
  waiting for transfers between devices: 67.5 us -> 0 us
  Pallas kernels: 33.9 us -> 79.8 us
  starting transfers between devices: 29.1 us -> 0 us
  between operations: 14.2 us -> 0.72 us
  local copies, waits for them, and re-layouts: 11.5 us -> 7.34 us
  other arithmetic: 1.78 us -> 0.06 us
    pallas_call x0 -> x2, Pallas kernels: none -> 50.6 us  [the longest x1 29.9 us: scatter(): pl.pallas_call(functools.partial(scatter_kernel, ranks, cols), out_shape=...]
    reduce_scatter x1 -> x0, waiting for transfers between devices: 38.7 us -> none  [per_device(): share = lax.psum_scatter(dkv, 'qrow', scatter_dimension=0, tiled=True)]
    all_to_all x8 -> x0, starting transfers between devices: 29 us -> none  [the longest x3 10.2 us: by_query(): x = lax.all_to_all(x.reshape(cols, part, LANES), 'kcol', 0, 0)]
    all_to_all x8 -> x0, waiting for transfers between devices: 28.8 us -> none  [the longest x3 13.6 us: by_query(): x = lax.all_to_all(x.reshape(cols, part, LANES), 'kcol', 0, 0)]
    reshape x9 -> x1, local copies, waits for them, and re-layouts: 5.24 us -> 0.09 us  [per_device(): query_at = lax.dynamic_slice(key_at.reshape(cols, ranks, halves, each), (...]
    pallas_call x1, Pallas kernels: 33.9 us -> 29.2 us  [attention(): pl.pallas_call(attention_kernel, out_shape=(jax.ShapeDtypeStruct(q.shape,...]
    unnamed x11 -> x15, local copies, waits for them, and re-layouts: 5.43 us -> 6.23 us
  transfers between devices with their start and end apart: 10 -> 0, of which waited for: 8 -> 0; matrix products, arithmetic and copies ran while one was open for 6% -> 0% of each run, Pallas kernels for 0% -> 0%
where the time goes in v2:
time: 88.2 us; the launch traced here: 87.9 us
  Pallas kernels  79.8 us (90%)
  local copies, waits for them, and re-layouts  7.34 us (8%)
    pallas_call x1, Pallas kernels, scatter(): pl.pallas_call(functools.partial(scatter_kernel, ranks, cols), out_shape=...  29.9 us
    pallas_call x1, Pallas kernels, attention(): pl.pallas_call(attention_kernel, out_shape=(jax.ShapeDtypeStruct(q.shape,...  29.2 us
    pallas_call x1, Pallas kernels, gather(): pl.pallas_call(functools.partial(gather_kernel, ranks, cols), out_shape=(...  20.7 us
    unnamed x15, local copies, waits for them, and re-layouts  6.23 us

profile of v2, /device:TPU:0, one launch (start us, length us, event | category | flops | bytes accessed | tf_op | source)
XLA Modules:
  0.0 87.9 jit_solution(4217903459215840838)
XLA Ops:
  0.6 0.0 copy-start.5
  0.6 0.8 reshape.83
  1.5 0.0 copy-start.4
  1.5 0.1 slice_reduce_fusion
  1.6 0.1 squeeze.6
  1.8 0.1 reshape.84.query_at
  1.9 0.0 copy-done.5
  1.9 0.5 copy-done.4
  2.3 0.0 copy-start.1
  2.3 0.9 %copy-done.1 = bf16[128,1024]{1,0:T(8,128)(2,1)S(1)} copy-done((bf16[128,1024]{1,0:T(8,128)(2,1)S(1)}, bf16[128,1024]{1,0:T(8,128)(2,1)}, u32[]{:S(2)}) %copy-start.1) | copy-done | bytes 262168
  3.3 0.0 copy-start.2
  3.3 0.9 %copy-done.2 = bf16[128,1024]{1,0:T(8,128)(2,1)S(1)} copy-done((bf16[128,1024]{1,0:T(8,128)(2,1)S(1)}, bf16[128,1024]{1,0:T(8,128)(2,1)}, u32[]{:S(2)}) %copy-start.2) | copy-done | bytes 262168
  4.2 0.0 copy-start.3
  4.2 0.9 %copy-done.3 = bf16[128,1024]{1,0:T(8,128)(2,1)S(1)} copy-done((bf16[128,1024]{1,0:T(8,128)(2,1)S(1)}, bf16[128,1024]{1,0:T(8,128)(2,1)}, u32[]{:S(2)}) %copy-start.3) | copy-done | bytes 262168
  5.2 20.7 %shard_map.85 = (bf16[512,256]{1,0:T(8,128)(2,1)S(1)}, bf16[512,256]{1,0:T(8,128)(2,1)S(1)}, f32[4,8,256]{2,1,0:T(8,128)S(1)}, bf16[4096,128]{1,0:T(8,128)(2,1)S(1)}) custom-call(bf16[128,1024]{1,0:T(8,128)(2,1)S(1)} %copy-done.1, bf16[128,1024]{1,0:T(8,128)(2,1)S(1)} %copy-done.2, bf16[128,1024]{1,0:T(8,128)(2,1)S(1)} %copy-done.3, ...), custom_call_target="tpu_custom_call" | custom-call | tf_op jit(solution)/shard_map/pallas_call | solution.py:282
  25.8 0.0 copy-start
  25.8 1.0 %copy-done = bf16[4096,128]{1,0:T(8,128)(2,1)} copy-done((bf16[4096,128]{1,0:T(8,128)(2,1)}, bf16[4096,128]{1,0:T(8,128)(2,1)S(1)}, u32[]{:S(2)}) %copy-start) | copy-done | bytes 1048600
  26.8 29.2 %shard_map.86 = (bf16[512,256]{1,0:T(8,128)(2,1)S(1)}, bf16[4096,128]{1,0:T(8,128)(2,1)S(1)}) custom-call(s32[64]{0:T(128)S(1)} %and_select_fusion.1.key_at, s32[8]{0:T(128)S(1)} %reshape.84.query_at, bf16[512,256]{1,0:T(8,128)(2,1)S(1)} %get-tuple-element.9.q_ref, bf16[512,256]{1,0:T(8,128)(2,1)S(1)} %get-tuple-element.10.g_ref, ...), custom_call_target="tpu_custom_call" | custom-call | tf_op jit(solution)/shard_map/pallas_call | solution.py:124
  56.0 29.9 %shard_map.87 = (bf16[128,1024]{1,0:T(8,128)(2,1)S(1)}, bf16[128,256]{1,0:T(8,128)(2,1)S(1)}, bf16[128,256]{1,0:T(8,128)(2,1)S(1)}) custom-call(bf16[512,256]{1,0:T(8,128)(2,1)S(1)} %get-tuple-element.13.dq_ref, bf16[4096,128]{1,0:T(8,128)(2,1)S(1)} %get-tuple-element.14.dkv_ref), custom_call_target="tpu_custom_call" | custom-call | tf_op jit(solution)/shard_map/pallas_call | solution.py:403
  85.9 0.7 copy.12
  86.6 0.6 copy.13
  87.3 0.6 copy.14
  (4 shorter events, 0.1 us)
Async XLA Ops:
  0.6 1.2 %copy-start.5 = (bf16[128,256]{1,0:T(8,128)(2,1)S(1)}, bf16[128,256]{1,0:T(8,128)(2,1)}, u32[]{:S(2)}) copy-start(bf16[128,256]{1,0:T(8,128)(2,1)} %v_ref.1) | copy-start | bytes 196612
  1.5 0.8 copy-start.4
  2.3 0.9 %copy-start.1 = (bf16[128,1024]{1,0:T(8,128)(2,1)S(1)}, bf16[128,1024]{1,0:T(8,128)(2,1)}, u32[]{:S(2)}) copy-start(bf16[128,1024]{1,0:T(8,128)(2,1)} %q_ref.1) | copy-start | bytes 786436
  3.3 0.9 %copy-start.2 = (bf16[128,1024]{1,0:T(8,128)(2,1)S(1)}, bf16[128,1024]{1,0:T(8,128)(2,1)}, u32[]{:S(2)}) copy-start(bf16[128,1024]{1,0:T(8,128)(2,1)} %g_ref.1) | copy-start | bytes 786436
  4.2 0.9 %copy-start.3 = (bf16[128,1024]{1,0:T(8,128)(2,1)S(1)}, bf16[128,1024]{1,0:T(8,128)(2,1)}, u32[]{:S(2)}) copy-start(bf16[128,1024]{1,0:T(8,128)(2,1)} %o_ref.1) | copy-start | bytes 786436
  25.8 1.0 %copy-start = (bf16[4096,128]{1,0:T(8,128)(2,1)}, bf16[4096,128]{1,0:T(8,128)(2,1)S(1)}, u32[]{:S(2)}) copy-start(bf16[4096,128]{1,0:T(8,128)(2,1)S(1)} %get-tuple-element.12.kv_ref) | copy-start | bytes 3145732

commit v3 on v2

--- a/solution.py
+++ b/solution.py
@@ -13,53 +13,65 @@
 STRETCH = 64
 MEMBERS = HEADS // KV_HEADS
 LANES = MEMBERS * STRETCH
-KB = 512
+KB = 1024
 
 
 def attention_kernel(
-    key_at, query_at, q_ref, g_ref, d_ref, kv_ref, dq_ref, dkv_ref,
-    kvs, kts, scr, acc, xq_t, xg_t, xq, xg,
+    ranks, cols, positions, q_ref, g_ref, d_ref, kv_ref, dq_ref, dkv_ref,
+    kvs, kts, scr, acc, xq_t, xg_t, xx,
 ):
     tokens = kv_ref.shape[0]
     stretches = tokens // STRETCH
     f32, bf16 = jnp.float32, jnp.bfloat16
+    rows = tokens // (ranks * cols)
+    halves = cols // KV_HEADS
+    part = rows // halves
+    each = part // STRETCH
+    rank = lax.axis_index("qrow")
+    half = lax.rem(lax.axis_index("kcol"), halves)
     lane = lax.broadcasted_iota(jnp.int32, (1, 2 * HEAD), 1)
-    each = q_ref.shape[0] // STRETCH // d_ref.shape[0]
 
     def place(t, c):
         src = pl.multiple_of(t * STRETCH, STRETCH)
-        dst = pl.multiple_of(key_at[t] * STRETCH, STRETCH)
+        dst = pl.multiple_of(positions[src], STRETCH)
         kvs[pl.ds(dst, STRETCH), :] = kv_ref[pl.ds(src, STRETCH), :]
         return c
 
-    lax.fori_loop(0, stretches, place, 0)
+    lax.fori_loop(0, stretches, place, 0, unroll=8)
 
     def turn(j, c):
-        rows = pl.multiple_of(j * KB, KB)
-        kts[j] = jnp.transpose(kvs[pl.ds(rows, KB), :])[HEAD:, :]
-        acc[pl.ds(rows, KB), :] = jnp.zeros((KB, 2 * HEAD), f32)
+        at = pl.multiple_of(j * KB, KB)
+        kts[j] = jnp.transpose(kvs[pl.ds(at, KB), :])[HEAD:, :]
+        acc[pl.ds(at, KB), :] = jnp.zeros((KB, 2 * HEAD), f32)
         return c
 
     lax.fori_loop(0, tokens // KB, turn, 0)
 
-    def by_head(block):
-        flat = jnp.transpose(block.astype(f32))
-        return jnp.concatenate([flat[h * HEAD : (h + 1) * HEAD] for h in range(MEMBERS)], axis=1)
+    def head_rows(block, upper):
+        pieces = []
+        for h in range(MEMBERS):
+            pair = block[:, (h // 2) * 2 * HEAD : (h // 2 + 1) * 2 * HEAD]
+            if (h % 2 == 1) != upper:
+                pair = pltpu.roll(pair, HEAD, 1)
+            pieces.append(jnp.where((lane >= HEAD) == upper, pair, 0.0))
+        return jnp.concatenate(pieces, axis=0)
 
     def one_stretch(st, c):
-        rows = pl.multiple_of(st * STRETCH, STRETCH)
-        at = query_at[st]
-        q_t = by_head(q_ref[pl.ds(rows, STRETCH), :]) * 0.125
-        g_t = by_head(g_ref[pl.ds(rows, STRETCH), :])
+        at = pl.multiple_of(st * STRETCH, STRETCH)
+        origin = ((st // each) * ranks + rank) * rows + half * part + lax.rem(st, each) * STRETCH
+        start = positions[origin]
+        g_rows = head_rows(g_ref[pl.ds(at, STRETCH), :].astype(f32), False)
+        q_rows = head_rows(q_ref[pl.ds(at, STRETCH), :].astype(f32) * 0.125, True)
         delta = d_ref[st // each, pl.ds(lax.rem(st, each), 1), :]
-        zero_t = jnp.zeros((HEAD, LANES), f32)
-        q_pad = jnp.concatenate([zero_t, q_t], axis=0)
-        g_pad = jnp.concatenate([g_t, zero_t], axis=0)
-        xq_t[...] = q_pad.astype(bf16)
-        xg_t[...] = g_pad.astype(bf16)
-        xq[...] = jnp.transpose(q_pad).astype(bf16)
-        xg[...] = jnp.transpose(g_pad).astype(bf16)
-        full = (at * STRETCH) // KB
+        xx[:LANES] = g_rows.astype(bf16)
+        xx[LANES:] = q_rows.astype(bf16)
+        turned = jnp.transpose(g_rows + q_rows).astype(bf16)
+        none = jnp.zeros((HEAD, LANES), bf16)
+        xg_t[:HEAD] = turned[:HEAD]
+        xg_t[HEAD:] = none
+        xq_t[:HEAD] = none
+        xq_t[HEAD:] = turned[HEAD:]
+        full = start // KB
 
         def scores(j):
             kr = pl.multiple_of(j * KB, KB)
@@ -75,8 +87,8 @@
 
         m = lax.fori_loop(0, full, first, jnp.full((8, LANES), -1e30, f32))
         kr, s = scores(full)
-        key_pos = kr + lax.broadcasted_iota(jnp.int32, (KB, LANES), 0)
-        row_pos = at * STRETCH + lax.rem(lax.broadcasted_iota(jnp.int32, (KB, LANES), 1), STRETCH)
+        key_pos = kr - start + lax.broadcasted_iota(jnp.int32, (KB, LANES), 0)
+        row_pos = lax.rem(lax.broadcasted_iota(jnp.int32, (1, LANES), 1), STRETCH)
         s = jnp.where(key_pos <= row_pos, s, -1e30)
         scr[pl.ds(kr, KB), :] = s
         m = jnp.max(fold_max(s, m), axis=0, keepdims=True)
@@ -95,14 +107,13 @@
             w = scr[pl.ds(kr, KB), :] * inverse
             dw = jnp.dot(kvs[pl.ds(kr, KB), :], xg_t[...], preferred_element_type=f32)
             ds = (w * (dw - delta)).astype(bf16)
-            acc[pl.ds(kr, KB), :] += jnp.dot(
-                w.astype(bf16), xg[...], preferred_element_type=f32
-            ) + jnp.dot(ds, xq[...], preferred_element_type=f32)
+            both = jnp.concatenate([w.astype(bf16), ds], axis=1)
+            acc[pl.ds(kr, KB), :] += jnp.dot(both, xx[...], preferred_element_type=f32)
             return dq + jnp.dot(kts[j], ds, preferred_element_type=f32)
 
         dq = lax.fori_loop(0, full + 1, third, jnp.zeros((HEAD, LANES), f32))
         flat = jnp.concatenate([dq[:, h * STRETCH : (h + 1) * STRETCH] for h in range(MEMBERS)], axis=0)
-        dq_ref[pl.ds(rows, STRETCH), :] = jnp.transpose(flat).astype(bf16)
+        dq_ref[pl.ds(at, STRETCH), :] = jnp.transpose(flat).astype(bf16)
         return c
 
     lax.fori_loop(0, q_ref.shape[0] // STRETCH, one_stretch, 0)
@@ -110,37 +121,37 @@
 
     def restore(t, c):
         dst = pl.multiple_of(t * STRETCH, STRETCH)
-        src = pl.multiple_of(key_at[t] * STRETCH, STRETCH)
+        src = pl.multiple_of(positions[dst], STRETCH)
         dkv_ref[pl.ds(dst, STRETCH), :] = (acc[pl.ds(src, STRETCH), :] * gain).astype(dkv_ref.dtype)
         return c
 
-    lax.fori_loop(0, stretches, restore, 0)
-
-
-def attention(key_at, query_at, q, g, d, kv, out_type):
+    lax.fori_loop(0, stretches, restore, 0, unroll=8)
+
+
+def attention(positions, q, g, d, kv, ranks, cols):
     tokens = kv.shape[0]
     vmem = pl.BlockSpec(memory_space=pltpu.VMEM)
     smem = pl.BlockSpec(memory_space=pltpu.SMEM)
+    bf16, f32 = jnp.bfloat16, jnp.float32
     return pl.pallas_call(
-        attention_kernel,
+        functools.partial(attention_kernel, ranks, cols),
         out_shape=(
-            jax.ShapeDtypeStruct(q.shape, jnp.bfloat16),
-            jax.ShapeDtypeStruct((tokens, 2 * HEAD), out_type),
+            jax.ShapeDtypeStruct(q.shape, bf16),
+            jax.ShapeDtypeStruct((tokens, 2 * HEAD), bf16),
         ),
-        in_specs=[smem, smem, vmem, vmem, vmem, vmem],
+        in_specs=[smem, vmem, vmem, vmem, vmem],
         out_specs=(vmem, vmem),
         scratch_shapes=[
-            pltpu.VMEM((tokens, 2 * HEAD), jnp.bfloat16),
-            pltpu.VMEM((tokens // KB, HEAD, KB), jnp.bfloat16),
-            pltpu.VMEM((tokens, LANES), jnp.float32),
-            pltpu.VMEM((tokens, 2 * HEAD), jnp.float32),
-            pltpu.VMEM((2 * HEAD, LANES), jnp.bfloat16),
-            pltpu.VMEM((2 * HEAD, LANES), jnp.bfloat16),
-            pltpu.VMEM((LANES, 2 * HEAD), jnp.bfloat16),
-            pltpu.VMEM((LANES, 2 * HEAD), jnp.bfloat16),
+            pltpu.VMEM((tokens, 2 * HEAD), bf16),
+            pltpu.VMEM((tokens // KB, HEAD, KB), bf16),
+            pltpu.VMEM((tokens, LANES), f32),
+            pltpu.VMEM((tokens, 2 * HEAD), f32),
+            pltpu.VMEM((2 * HEAD, LANES), bf16),
+            pltpu.VMEM((2 * HEAD, LANES), bf16),
+            pltpu.VMEM((2 * LANES, 2 * HEAD), bf16),
         ],
         compiler_params=pltpu.CompilerParams(vmem_limit_bytes=52 * 1024 * 1024),
-    )(key_at, query_at, q, g, d, kv)
+    )(positions, q, g, d, kv)
 
 
 def greet(ranks, cols):
@@ -171,17 +182,20 @@
 
 
 def gather_kernel(
-    ranks, cols, q_ref, g_ref, o_ref, k_ref, v_ref, q_out, g_out, d_out, kv_out,
-    packed, terms, send_a, recv_a, send_z, recv_z, send_s, recv_s,
+    ranks, cols, q_any, g_any, o_any, k_any, v_any, q_out, g_out, d_out, kv_out,
+    packed, terms, g_ref, o_ref, k_ref, v_ref, fetched, send_a, recv_a, send_z, recv_z, send_s, recv_s,
 ):
     f32, bf16 = jnp.float32, jnp.bfloat16
     r, c = lax.axis_index("qrow"), lax.axis_index("kcol")
     sibling = r + 1 - 2 * lax.rem(r, 2)
-    rows = q_ref.shape[0]
+    rows = q_any.shape[0]
     halves = cols // KV_HEADS
     part = rows // halves
     block = cols * rows
-    greet(ranks, cols)
+    pairs = [(k_any, k_ref), (v_any, v_ref), (g_any, g_ref), (o_any, o_ref)]
+    fetches = [pltpu.make_async_copy(a, b, fetched.at[n]) for n, (a, b) in enumerate(pairs)]
+    for fetch in fetches:
+        fetch.start()
 
     def key_rows(rank, col):
         return pl.ds(pl.multiple_of((rank * cols + col) * rows, rows), rows)
@@ -193,12 +207,21 @@
         half = pl.ds(pl.multiple_of(lax.rem(col, halves) * part, part), part)
         return half, pl.ds(pl.multiple_of((col // halves) * LANES, LANES), LANES)
 
+    half, columns = query_slice(c)
+    own_query = pltpu.make_async_copy(
+        q_any.at[half, columns], q_out.at[query_rows(c)], fetched.at[4]
+    )
+    own_query.start()
+    fetches[0].wait()
+    fetches[1].wait()
     for h in range(KV_HEADS):
         cut = slice(h * HEAD, (h + 1) * HEAD)
         packed[h] = jnp.concatenate(
             [(v_ref[:, cut].astype(f32) * 0.125).astype(bf16), k_ref[:, cut]], axis=1
         )
 
+    greet(ranks, cols)
+
     def to_peer(k, which, src, dst, peer):
         return remote(src, dst, send_a.at[k, which], recv_a.at[k, which], (r, peer))
 
@@ -211,7 +234,7 @@
         copies[-1].start()
     for k in range(1, cols):
         peer = lax.rem(c + k, cols)
-        for which, (src, dst) in enumerate([(q_ref, q_out), (g_ref, g_out)]):
+        for which, (src, dst) in enumerate([(q_any, q_out), (g_any, g_out)]):
             half, columns = query_slice(peer)
             copies.append(
                 to_peer(k, 1 + which, src.at[half, columns], dst.at[query_rows(c)], peer)
@@ -219,7 +242,9 @@
             copies[-1].start()
     kv_out[key_rows(r, c), :] = packed[c // halves]
     half, columns = query_slice(c)
-    q_out[query_rows(c), :] = q_ref[half, columns]
+    fetches[2].wait()
+    fetches[3].wait()
+    own_query.wait()
     g_out[query_rows(c), :] = g_ref[half, columns]
 
     for h in range(KV_HEADS):
@@ -287,11 +312,16 @@
             jax.ShapeDtypeStruct((cols, 8, LANES), jnp.float32),
             jax.ShapeDtypeStruct((ranks * cols * rows, 2 * HEAD), bf16),
         ),
-        in_specs=[vmem] * 5,
+        in_specs=[pl.BlockSpec(memory_space=pltpu.HBM)] * 5,
         out_specs=(vmem,) * 4,
         scratch_shapes=[
             pltpu.VMEM((KV_HEADS, rows, 2 * HEAD), bf16),
             pltpu.VMEM((cols, 8, LANES), jnp.float32),
+            pltpu.VMEM((rows, HEADS * HEAD), bf16),
+            pltpu.VMEM((rows, HEADS * HEAD), bf16),
+            pltpu.VMEM((rows, KV_HEADS * HEAD), bf16),
+            pltpu.VMEM((rows, KV_HEADS * HEAD), bf16),
+            dma((5,)),
             dma((cols, 4)), dma((cols, 4)),
             dma((ranks // 2,)), dma((ranks // 2,)),
             dma((ranks // 2,)), dma((ranks // 2,)),
@@ -430,16 +460,8 @@
     rows = queries.shape[0]
     ranks = lax.axis_size("qrow")
     cols = lax.axis_size("kcol")
-    halves = cols // KV_HEADS
-    each = rows // halves // STRETCH
-    mine = lax.axis_index("qrow")
-    half = lax.rem(lax.axis_index("kcol"), halves)
-    key_at = positions.reshape(-1, STRETCH)[:, 0] // STRETCH
-    query_at = lax.dynamic_slice(
-        key_at.reshape(cols, ranks, halves, each), (0, mine, half, 0), (cols, 1, 1, each)
-    ).reshape(-1)
     q, g, d, kv = gather(queries, out_grad, outputs, keys, values, ranks, cols)
-    dq, dkv = attention(key_at, query_at, q, g, d, kv, jnp.bfloat16)
+    dq, dkv = attention(positions, q, g, d, kv, ranks, cols)
     return scatter(dq, dkv, rows, ranks, cols)
 
 

time: 88.2 us -> 78.3 us (0.89)
  Pallas kernels: 79.8 us -> 69.2 us
    pallas_call x1, Pallas kernels: 29.9 us -> 21.8 us  [scatter(): pl.pallas_call(functools.partial(scatter_kernel, ranks, cols), out_shape=...]
    pallas_call x1, Pallas kernels: 29.2 us -> 26.5 us  [attention(): pl.pallas_call(functools.partial(attention_kernel, ranks, cols), out_shap...]
    unnamed x15 -> x17, local copies, waits for them, and re-layouts: 6.23 us -> 7.44 us
    reshape x2 -> x0, local copies, waits for them, and re-layouts: 0.9 us -> none  [the longest x1 0.82 us: per_device(): key_at = positions.reshape(-1, STRETCH)[:, 0] // STRETCH]
where the time goes in v3:
time: 78.3 us; the launch traced here: 77.3 us
  Pallas kernels  69.2 us (88%)
  local copies, waits for them, and re-layouts  7.44 us (10%)
    pallas_call x1, Pallas kernels, attention(): pl.pallas_call(functools.partial(attention_kernel, ranks, cols), out_shap...  26.5 us
    pallas_call x1, Pallas kernels, scatter(): pl.pallas_call(functools.partial(scatter_kernel, ranks, cols), out_shape=...  21.8 us
    pallas_call x1, Pallas kernels, gather(): pl.pallas_call(functools.partial(gather_kernel, ranks, cols), out_shape=(...  20.9 us
    unnamed x17, local copies, waits for them, and re-layouts  7.44 us

profile of v3, /device:TPU:0, one launch (start us, length us, event | category | flops | bytes accessed | tf_op | source)
XLA Modules:
  0.0 77.3 jit_solution(9992436975966401056)
XLA Ops:
  0.6 0.0 copy-start.1
  0.6 0.9 %copy-done.1 = bf16[128,1024]{1,0:T(8,128)(2,1)S(1)} copy-done((bf16[128,1024]{1,0:T(8,128)(2,1)S(1)}, bf16[128,1024]{1,0:T(8,128)(2,1)}, u32[]{:S(2)}) %copy-start.1) | copy-done | bytes 262168
  1.6 0.0 copy-start.2
  1.6 0.9 %copy-done.2 = bf16[128,1024]{1,0:T(8,128)(2,1)S(1)} copy-done((bf16[128,1024]{1,0:T(8,128)(2,1)S(1)}, bf16[128,1024]{1,0:T(8,128)(2,1)}, u32[]{:S(2)}) %copy-start.2) | copy-done | bytes 262168
  2.5 0.0 copy-start.3
  2.5 0.9 %copy-done.3 = bf16[128,1024]{1,0:T(8,128)(2,1)S(1)} copy-done((bf16[128,1024]{1,0:T(8,128)(2,1)S(1)}, bf16[128,1024]{1,0:T(8,128)(2,1)}, u32[]{:S(2)}) %copy-start.3) | copy-done | bytes 262168
  3.5 0.0 copy-start.4
  3.5 0.8 %copy-done.4 = bf16[128,256]{1,0:T(8,128)(2,1)S(1)} copy-done((bf16[128,256]{1,0:T(8,128)(2,1)S(1)}, bf16[128,256]{1,0:T(8,128)(2,1)}, u32[]{:S(2)}) %copy-start.4) | copy-done | bytes 65560
  4.3 0.0 copy-start.5
  4.3 0.8 %copy-done.5 = bf16[128,256]{1,0:T(8,128)(2,1)S(1)} copy-done((bf16[128,256]{1,0:T(8,128)(2,1)S(1)}, bf16[128,256]{1,0:T(8,128)(2,1)}, u32[]{:S(2)}) %copy-start.5) | copy-done | bytes 65560
  5.2 0.0 copy-start.6
  5.2 20.9 %shard_map.85 = (bf16[512,256]{1,0:T(8,128)(2,1)S(1)}, bf16[512,256]{1,0:T(8,128)(2,1)S(1)}, f32[4,8,256]{2,1,0:T(8,128)S(1)}, bf16[4096,128]{1,0:T(8,128)(2,1)S(1)}) custom-call(bf16[128,1024]{1,0:T(8,128)(2,1)S(1)} %copy-done.1, bf16[128,1024]{1,0:T(8,128)(2,1)S(1)} %copy-done.2, bf16[128,1024]{1,0:T(8,128)(2,1)S(1)} %copy-done.3, ...), custom_call_target="tpu_custom_call" | custom-call | tf_op jit(solution)/shard_map/pallas_call | solution.py:307
  26.1 0.0 copy-start
  26.1 1.0 %copy-done = bf16[4096,128]{1,0:T(8,128)(2,1)} copy-done((bf16[4096,128]{1,0:T(8,128)(2,1)}, bf16[4096,128]{1,0:T(8,128)(2,1)S(1)}, u32[]{:S(2)}) %copy-start) | copy-done | bytes 1048600
  27.1 0.0 copy-done.6
  27.1 26.5 %shard_map.86 = (bf16[512,256]{1,0:T(8,128)(2,1)S(1)}, bf16[4096,128]{1,0:T(8,128)(2,1)S(1)}) custom-call(s32[4096]{0:T(1024)S(1)} %copy-done.6, bf16[512,256]{1,0:T(8,128)(2,1)S(1)} %get-tuple-element.9.q_ref, bf16[512,256]{1,0:T(8,128)(2,1)S(1)} %get-tuple-element.10.g_ref, f32[4,8,256]{2,1,0:T(8,128)S(1)} %get-tuple-element.11.d_ref, ...), custom_call_target="tpu_custom_call" | custom-call | tf_op jit(solution)/shard_map/pallas_call | solution.py:136
  53.5 21.8 %shard_map.87 = (bf16[128,1024]{1,0:T(8,128)(2,1)S(1)}, bf16[128,256]{1,0:T(8,128)(2,1)S(1)}, bf16[128,256]{1,0:T(8,128)(2,1)S(1)}) custom-call(bf16[512,256]{1,0:T(8,128)(2,1)S(1)} %get-tuple-element.13.dq_ref, bf16[4096,128]{1,0:T(8,128)(2,1)S(1)} %get-tuple-element.14.dkv_ref), custom_call_target="tpu_custom_call" | custom-call | tf_op jit(solution)/shard_map/pallas_call | solution.py:433
  75.3 0.7 copy.12
  76.1 0.6 copy.13
  76.7 0.6 copy.14
Async XLA Ops:
  0.6 1.0 %copy-start.1 = (bf16[128,1024]{1,0:T(8,128)(2,1)S(1)}, bf16[128,1024]{1,0:T(8,128)(2,1)}, u32[]{:S(2)}) copy-start(bf16[128,1024]{1,0:T(8,128)(2,1)} %q_any.1) | copy-start | bytes 786436
  1.6 0.9 %copy-start.2 = (bf16[128,1024]{1,0:T(8,128)(2,1)S(1)}, bf16[128,1024]{1,0:T(8,128)(2,1)}, u32[]{:S(2)}) copy-start(bf16[128,1024]{1,0:T(8,128)(2,1)} %g_any.1) | copy-start | bytes 786436
  2.5 0.9 %copy-start.3 = (bf16[128,1024]{1,0:T(8,128)(2,1)S(1)}, bf16[128,1024]{1,0:T(8,128)(2,1)}, u32[]{:S(2)}) copy-start(bf16[128,1024]{1,0:T(8,128)(2,1)} %o_any.1) | copy-start | bytes 786436
  3.5 0.8 %copy-start.4 = (bf16[128,256]{1,0:T(8,128)(2,1)S(1)}, bf16[128,256]{1,0:T(8,128)(2,1)}, u32[]{:S(2)}) copy-start(bf16[128,256]{1,0:T(8,128)(2,1)} %k_any.1) | copy-start | bytes 196612
  4.3 0.8 %copy-start.5 = (bf16[128,256]{1,0:T(8,128)(2,1)S(1)}, bf16[128,256]{1,0:T(8,128)(2,1)}, u32[]{:S(2)}) copy-start(bf16[128,256]{1,0:T(8,128)(2,1)} %v_any.1) | copy-start | bytes 196612
  5.2 21.9 %copy-start.6 = (s32[4096]{0:T(1024)S(1)}, s32[4096]{0:T(1024)}, u32[]{:S(2)}) copy-start(s32[4096]{0:T(1024)} %positions.1) | copy-start | bytes 49156
  26.1 1.0 %copy-start = (bf16[4096,128]{1,0:T(8,128)(2,1)}, bf16[4096,128]{1,0:T(8,128)(2,1)S(1)}, u32[]{:S(2)}) copy-start(bf16[4096,128]{1,0:T(8,128)(2,1)S(1)} %get-tuple-element.12.kv_ref) | copy-start | bytes 3145732
